TPU v7x, 128 devices: a whole 4x4x4 slice. The times are simulated.
128 devices in a mesh: ctx: 32 (over z, x, core), col: 4 (over y).
Axes of the slice: x: 4, y: 4, z: 4, core: 2. Of those that a mesh axis runs over, the one named last changes fastest.
Arguments:
- sequence: bfloat16 [16384, 4096], P('ctx', 'col'), may hold values from -6 to 6
- w_proj: bfloat16 [4096, 3, 2048], P('col'), may hold values from -0.125 to 0.125
- short_filter: float32 [3, 3, 2048], P(None, None, 'col'), may hold values from -3 to 3
- long_filter: float32 [16384, 2048], P('ctx', 'col'), may hold values from -0.046875 to 0.046875
- skip_gain: float32 [2048], P('col'), may hold values from 0.5 to 1.5
Outputs:
- mixed: float32 [16384, 2048], P('ctx', 'col')
All inputs are finite; a program needn't handle non-finite values.
Results may differ from a plain program's by a relative error of at most 0.0003.
Values sent between devices are 32-bit elements; how exact they have to be, the bound alone decides.
A program may use at most 128 MiB of HBM per device.

v0:
```python
import math

import jax
import jax.numpy as jnp
from jax import lax
from jax.sharding import PartitionSpec as P

RADIX = 32


def swapped(x, axis, bit):
    return lax.ppermute(x, axis, [(i, i ^ 1 << bit) for i in range(lax.axis_size(axis))])


def passed_along(block, axis, distance):
    devices = range(lax.axis_size(axis))
    route = [((i - distance) % len(devices), i) for i in devices]
    return lax.ppermute(block, axis, route)


def twiddles(length, sign):
    steps_row = jnp.arange(length, dtype=jnp.int32)
    product = steps_row[:, None] * steps_row[None, :] % length
    phase_angle = sign * 2.0 * math.pi / length * product.astype(jnp.float32)
    return (jnp.cos(phase_angle), jnp.sin(phase_angle))


def twiddle_grid(first_count, second_count, modulus, sign):
    first_steps = jnp.arange(first_count, dtype=jnp.int32)
    second_steps = jnp.arange(second_count, dtype=jnp.int32)
    product = first_steps[:, None] * second_steps[None, :]
    phase_angle = sign * 2.0 * math.pi / modulus * product.astype(jnp.float32)
    return (jnp.cos(phase_angle), jnp.sin(phase_angle))


def complex_product(left_real, left_imag, right_real, right_imag):
    return (
        left_real * right_real - left_imag * right_imag,
        left_real * right_imag + left_imag * right_real,
    )


def complex_apply(pattern, table_pair, real_part, imag_part):
    stacked = jnp.stack([real_part, imag_part])
    with_cos = jnp.einsum(pattern, table_pair[0], stacked, precision=lax.Precision.HIGHEST)
    with_sin = jnp.einsum(pattern, table_pair[1], stacked, precision=lax.Precision.HIGHEST)
    return (with_cos[0] - with_sin[1], with_cos[1] + with_sin[0])


def local_forward(real_part, imag_part):
    signal_count, rows_here, channel_width = real_part.shape
    second_radix = rows_here // RADIX
    split_shape = (signal_count, RADIX, second_radix, channel_width)
    real_part, imag_part = complex_apply(
        "ar,zkrsc->zkasc",
        twiddles(RADIX, -1.0),
        real_part.reshape(split_shape),
        imag_part.reshape(split_shape),
    )
    inner_cos, inner_sin = twiddle_grid(RADIX, second_radix, rows_here, -1.0)
    real_part, imag_part = complex_product(
        real_part, imag_part, inner_cos[:, :, None], inner_sin[:, :, None]
    )
    return complex_apply("bs,zkasc->zkabc", twiddles(second_radix, -1.0), real_part, imag_part)


def local_inverse(real_part, imag_part):
    signal_count, first_count, second_radix, channel_width = real_part.shape
    rows_here = first_count * second_radix
    real_part, imag_part = complex_apply(
        "sb,zkabc->zkasc", twiddles(second_radix, 1.0), real_part, imag_part
    )
    inner_cos, inner_sin = twiddle_grid(first_count, second_radix, rows_here, 1.0)
    real_part, imag_part = complex_product(
        real_part, imag_part, inner_cos[:, :, None], inner_sin[:, :, None]
    )
    real_part, imag_part = complex_apply(
        "ra,zkasc->zkrsc", twiddles(first_count, 1.0), real_part, imag_part
    )
    return (
        real_part.reshape(signal_count, rows_here, channel_width),
        imag_part.reshape(signal_count, rows_here, channel_width),
    )


def global_turn(real_part, imag_part, frequency, total_length, sign):
    rows_here = real_part.shape[1]
    product = jnp.arange(rows_here, dtype=jnp.int32) * frequency
    phase_angle = sign * 2.0 * math.pi / total_length * product.astype(jnp.float32)
    return complex_product(
        real_part, imag_part, jnp.cos(phase_angle)[:, None], jnp.sin(phase_angle)[:, None]
    )


def reversed_bits(position, levels):
    result = jnp.zeros((), jnp.int32)
    for shift_at in range(levels):
        picked = jnp.bitwise_and(jnp.right_shift(position, shift_at), 1)
        result = result + jnp.left_shift(picked, levels - 1 - shift_at)
    return result


def pair_setup(position, section_bit, sign):
    half_span = 1 << section_bit
    offset_low = jnp.bitwise_and(position, half_span - 1)
    bottom = jnp.bitwise_and(jnp.right_shift(position, section_bit), 1) == 1
    phase_angle = sign * 2.0 * math.pi / (2 * half_span) * offset_low.astype(jnp.float32)
    return (bottom, jnp.cos(phase_angle), jnp.sin(phase_angle))


def forward_butterfly(signal):
    position = lax.axis_index("ctx")
    levels = lax.axis_size("ctx").bit_length() - 1
    bottom, cosine, sine = pair_setup(position, levels - 1, -1.0)
    partner = swapped(signal, "ctx", levels - 1)
    difference = partner - signal
    real_part = jnp.where(bottom, difference * cosine, signal + partner)
    imag_part = jnp.where(bottom, difference * sine, jnp.zeros_like(signal))
    for section_bit in range(levels - 2, -1, -1):
        bottom, cosine, sine = pair_setup(position, section_bit, -1.0)
        partner_real, partner_imag = swapped((real_part, imag_part), "ctx", section_bit)
        turned_real, turned_imag = complex_product(
            partner_real - real_part, partner_imag - imag_part, cosine, sine
        )
        real_part = jnp.where(bottom, turned_real, real_part + partner_real)
        imag_part = jnp.where(bottom, turned_imag, imag_part + partner_imag)
    return (real_part, imag_part, reversed_bits(position, levels))


def inverse_butterfly(real_part, imag_part):
    position = lax.axis_index("ctx")
    levels = lax.axis_size("ctx").bit_length() - 1
    for section_bit in range(levels - 1):
        bottom, cosine, sine = pair_setup(position, section_bit, 1.0)
        turned_real, turned_imag = complex_product(real_part, imag_part, cosine, sine)
        sent_real = jnp.where(bottom, turned_real, real_part)
        sent_imag = jnp.where(bottom, turned_imag, imag_part)
        partner_real, partner_imag = swapped((sent_real, sent_imag), "ctx", section_bit)
        real_part = jnp.where(bottom, partner_real - sent_real, sent_real + partner_real)
        imag_part = jnp.where(bottom, partner_imag - sent_imag, sent_imag + partner_imag)
    bottom, cosine, sine = pair_setup(position, levels - 1, 1.0)
    sent_real = jnp.where(bottom, real_part * cosine - imag_part * sine, real_part)
    partner_real = swapped(sent_real, "ctx", levels - 1)
    return jnp.where(bottom, partner_real - sent_real, sent_real + partner_real)


def on_device(sequence, w_proj, short_filter, long_filter, skip_gain):
    rows_here = sequence.shape[0]
    channels_all = w_proj.shape[2]
    total_length = rows_here * lax.axis_size("ctx")
    partial_sums = jnp.dot(
        sequence,
        w_proj.reshape(w_proj.shape[0], 3 * channels_all),
        preferred_element_type=jnp.float32,
    )
    projected = lax.psum_scatter(
        partial_sums.reshape(rows_here, 3, channels_all), "col", scatter_dimension=2, tiled=True
    )
    rim_rows = passed_along(projected[rows_here - 2 :], "ctx", 1)
    padded = jnp.concatenate([rim_rows, projected], axis=0)
    shaped = (
        short_filter[0] * projected
        + short_filter[1] * padded[1 : rows_here + 1]
        + short_filter[2] * padded[0:rows_here]
    )
    query_rows = shaped[:, 0, :]
    gated_values = shaped[:, 1, :] * shaped[:, 2, :]
    signal = jnp.stack([gated_values, long_filter])
    real_part, imag_part, frequency = forward_butterfly(signal)
    real_part, imag_part = global_turn(real_part, imag_part, frequency, total_length, -1.0)
    real_part, imag_part = local_forward(real_part, imag_part)
    prod_real, prod_imag = complex_product(
        real_part[0:1], imag_part[0:1], real_part[1:2], imag_part[1:2]
    )
    real_part, imag_part = local_inverse(prod_real, prod_imag)
    real_part, imag_part = global_turn(real_part, imag_part, frequency, total_length, 1.0)
    combined = inverse_butterfly(real_part, imag_part)
    convolved = combined[0] / total_length
    return query_rows * (convolved + skip_gain * gated_values)


def solution(mesh):
    return jax.shard_map(
        on_device,
        mesh=mesh,
        in_specs=(
            P("ctx", "col"),
            P("col", None, None),
            P(None, None, "col"),
            P("ctx", "col"),
            P("col"),
        ),
        out_specs=P("ctx", "col"),
        check_vma=False,
    )
```

profile of v0, /device:TPU:0, one launch (start us, length us, event | category | flops | bytes accessed | tf_op | source)
XLA Modules:
  0.0 757.8 jit_solution(4504260927616640676)
XLA Ops:
  6.5 16.7 %copy.16 = bf16[1024,3,2048]{0,2,1:T(8,128)(2,1)} copy(bf16[1024,3,2048]{2,0,1:T(8,128)(2,1)} %param.6) | data formatting | bytes 25165824 | tf_op args[1]
  23.3 19.4 %fusion = f32[512,3,2048]{2,0,1:T(8,128)} fusion(bf16[1024,3,2048]{0,2,1:T(8,128)(2,1)} %copy.16, bf16[512,1024]{1,0:T(8,128)(2,1)S(1)} %copy-done), kind=kOutput, calls=%fused_computation | convolution fusion | flops 6442450944 | bytes 26214400 | tf_op jit(solution)/shard_map/dot_general | solution.py:151
  42.7 117.1 %reduce-scatter.2.cloned.1.call-done = f32[512,3,512]{2,0,1:T(8,128)} async-done(((f32[512,3,2048]{2,0,1:T(8,128)}), f32[512,3,512]{2,0,1:T(8,128)}) %reduce-scatter.2.cloned.1.call-update) | async-done | bytes 3145744 | tf_op jit(solution)/shard_map/reduce_scatter | solution.py:156
  160.7 6.4 collective-permute-done
  167.1 5.0 fusion.9
  176.5 43.0 %collective-permute-done.1 = f32[2,512,512]{2,1,0:T(8,128)} collective-permute-done((f32[2,512,512]{2,1,0:T(8,128)S(1)}, f32[2,512,512]{2,1,0:T(8,128)}, u32[]{:S(2)}, u32[]{:S(2)}) %collective-permute-start.1) | collective-permute-done | bytes 2097184 | tf_op jit(solution)/shard_map/ppermute | solution.py:12
  219.5 3.9 multiply_select_fusion
  225.6 46.5 %collective-permute-done.3 = f32[2,512,512]{2,1,0:T(8,128)} collective-permute-done((f32[2,512,512]{2,1,0:T(8,128)S(1)}, f32[2,512,512]{2,1,0:T(8,128)}, u32[]{:S(2)}, u32[]{:S(2)}) %collective-permute-start.3) | collective-permute-done | bytes 2097184 | tf_op jit(solution)/shard_map/ppermute | solution.py:12
  272.1 40.0 %collective-permute-done.2 = f32[2,512,512]{2,1,0:T(8,128)} collective-permute-done((f32[2,512,512]{2,1,0:T(8,128)}, f32[2,512,512]{2,1,0:T(8,128)}, u32[]{:S(2)}, u32[]{:S(2)}) %collective-permute-start.2) | collective-permute-done | bytes 2097184 | tf_op jit(solution)/shard_map/ppermute | solution.py:12
  312.1 6.1 add_select_fusion.6
  318.2 4.7 collective-permute-start.5
  323.1 46.5 %collective-permute-done.5 = f32[2,512,512]{2,1,0:T(8,128)} collective-permute-done((f32[2,512,512]{2,1,0:T(8,128)S(1)}, f32[2,512,512]{2,1,0:T(8,128)}, u32[]{:S(2)}, u32[]{:S(2)}) %collective-permute-start.5) | collective-permute-done | bytes 2097184 | tf_op jit(solution)/shard_map/ppermute | solution.py:12
  369.5 41.3 %collective-permute-done.4 = f32[2,512,512]{2,1,0:T(8,128)} collective-permute-done((f32[2,512,512]{2,1,0:T(8,128)}, f32[2,512,512]{2,1,0:T(8,128)}, u32[]{:S(2)}, u32[]{:S(2)}) %collective-permute-start.4) | collective-permute-done | bytes 2097184 | tf_op jit(solution)/shard_map/ppermute | solution.py:12
  410.9 6.0 add_select_fusion.4
  419.7 46.6 %collective-permute-done.7 = f32[2,512,512]{2,1,0:T(8,128)S(1)} collective-permute-done((f32[2,512,512]{2,1,0:T(8,128)}, f32[2,512,512]{2,1,0:T(8,128)S(1)}, u32[]{:S(2)}, u32[]{:S(2)}) %collective-permute-start.7) | collective-permute-done | bytes 2097184 | tf_op jit(solution)/shard_map/ppermute | solution.py:12
  467.5 39.5 %collective-permute-done.6 = f32[2,512,512]{2,1,0:T(8,128)} collective-permute-done((f32[2,512,512]{2,1,0:T(8,128)}, f32[2,512,512]{2,1,0:T(8,128)}, u32[]{:S(2)}, u32[]{:S(2)}) %collective-permute-start.6) | collective-permute-done | bytes 2097184 | tf_op jit(solution)/shard_map/ppermute | solution.py:12
  507.0 6.1 add_select_fusion.2
  514.4 5.6 collective-permute-done.8
  520.8 3.8 multiply_add_fusion.1
  527.3 4.4 convolution_bitcast_fusion
  531.8 4.7 convolution_bitcast_fusion.1
  537.7 6.8 fusion.14
  544.5 7.1 fusion.11
  558.5 3.6 fusion.28
  577.3 24.0 %collective-permute-done.12 = f32[1,512,512]{2,1,0:T(8,128)S(1)} collective-permute-done((f32[1,512,512]{2,1,0:T(8,128)}, f32[1,512,512]{2,1,0:T(8,128)S(1)}, u32[]{:S(2)}, u32[]{:S(2)}) %collective-permute-start.12) | collective-permute-done | bytes 1048608 | tf_op jit(solution)/shard_map/ppermute | solution.py:12
  602.3 20.8 %collective-permute-done.13 = f32[1,512,512]{2,1,0:T(8,128)} collective-permute-done((f32[1,512,512]{2,1,0:T(8,128)S(1)}, f32[1,512,512]{2,1,0:T(8,128)}, u32[]{:S(2)}, u32[]{:S(2)}) %collective-permute-start.13) | collective-permute-done | bytes 1048608 | tf_op jit(solution)/shard_map/ppermute | solution.py:12
  629.3 23.9 %collective-permute-done.14 = f32[1,512,512]{2,1,0:T(8,128)S(1)} collective-permute-done((f32[1,512,512]{2,1,0:T(8,128)S(1)}, f32[1,512,512]{2,1,0:T(8,128)S(1)}, u32[]{:S(2)}, u32[]{:S(2)}) %collective-permute-start.14) | collective-permute-done | bytes 1048608 | tf_op jit(solution)/shard_map/ppermute | solution.py:12
  653.3 20.9 %collective-permute-done.15 = f32[1,512,512]{2,1,0:T(8,128)} collective-permute-done((f32[1,512,512]{2,1,0:T(8,128)S(1)}, f32[1,512,512]{2,1,0:T(8,128)}, u32[]{:S(2)}, u32[]{:S(2)}) %collective-permute-start.15) | collective-permute-done | bytes 1048608 | tf_op jit(solution)/shard_map/ppermute | solution.py:12
  678.8 23.9 %collective-permute-done.17 = f32[1,512,512]{2,1,0:T(8,128)S(1)} collective-permute-done((f32[1,512,512]{2,1,0:T(8,128)S(1)}, f32[1,512,512]{2,1,0:T(8,128)S(1)}, u32[]{:S(2)}, u32[]{:S(2)}) %collective-permute-start.17) | collective-permute-done | bytes 1048608 | tf_op jit(solution)/shard_map/ppermute | solution.py:12
  703.7 19.0 %collective-permute-done.16 = f32[1,512,512]{2,1,0:T(8,128)} collective-permute-done((f32[1,512,512]{2,1,0:T(8,128)S(1)}, f32[1,512,512]{2,1,0:T(8,128)}, u32[]{:S(2)}, u32[]{:S(2)}) %collective-permute-start.16) | collective-permute-done | bytes 1048608 | tf_op jit(solution)/shard_map/ppermute | solution.py:12
  724.8 3.3 collective-permute-start.18
  728.1 20.8 %collective-permute-done.18 = f32[1,512,512]{2,1,0:T(8,128)S(1)} collective-permute-done((f32[1,512,512]{2,1,0:T(8,128)S(1)}, f32[1,512,512]{2,1,0:T(8,128)S(1)}, u32[]{:S(2)}, u32[]{:S(2)}) %collective-permute-start.18) | collective-permute-done | bytes 1048608 | tf_op jit(solution)/shard_map/ppermute | solution.py:12
  (82 shorter events, 55.0 us)
Async XLA Ops:
  6.5 16.7 %copy-start = (bf16[512,1024]{1,0:T(8,128)(2,1)S(1)}, bf16[512,1024]{1,0:T(8,128)(2,1)}, u32[]{:S(2)}) copy-start(bf16[512,1024]{1,0:T(8,128)(2,1)} %param.5) | copy-start | bytes 3145732
  6.5 153.3 %reduce-scatter.2.cloned.1.call-start = ((), (), s32[]{:S(2)}) async-start(), calls=%async_computation.1 | async-start | bytes 15728640 | tf_op jit(solution)/shard_map/reduce_scatter | solution.py:156
  42.7 118.0 %copy-start.12 = (f32[3,3,512]{2,1,0:T(4,128)S(1)}, f32[3,3,512]{2,1,0:T(4,128)}, u32[]{:S(2)}) copy-start(f32[3,3,512]{2,1,0:T(4,128)} %param.7) | copy-start | bytes 55300
  160.7 6.4 collective-permute-start
  172.1 2.2 copy-start.2
  172.1 2.0 copy-start.5
  174.3 45.2 %collective-permute-start.1 = (f32[2,512,512]{2,1,0:T(8,128)S(1)}, f32[2,512,512]{2,1,0:T(8,128)}, u32[]{:S(2)}, u32[]{:S(2)}) collective-permute-start(f32[2,512,512]{2,1,0:T(8,128)S(1)} %pad_maximum_fusion.2), channel_id=1, source_target_pairs={{0,64},{4,68},{8,72},{12,76},{16,80},{20,84},{24,88},{28,92},{32,9... | collective-permute-start | bytes 6291464 | tf_op jit(solution)/shard_map/ppermute | solution.py:12
  223.4 48.7 %copy-start.4 = (f32[2,512,512]{2,1,0:T(8,128)}, f32[2,512,512]{2,1,0:T(8,128)S(1)}, u32[]{:S(2)}) copy-start(f32[2,512,512]{2,1,0:T(8,128)S(1)} %get-tuple-element.30) | copy-start | bytes 6291460
  223.4 48.7 %collective-permute-start.3 = (f32[2,512,512]{2,1,0:T(8,128)S(1)}, f32[2,512,512]{2,1,0:T(8,128)}, u32[]{:S(2)}, u32[]{:S(2)}) collective-permute-start(f32[2,512,512]{2,1,0:T(8,128)S(1)} %get-tuple-element.30), channel_id=1, source_target_pairs={{0,32},{4,36},{8,40},{12,44},{16,48},{20,52},{24,56},{28,60},{32,0... | collective-permute-start | bytes 6291464 | tf_op jit(solution)/shard_map/ppermute | solution.py:12
  225.0 87.1 %collective-permute-start.2 = (f32[2,512,512]{2,1,0:T(8,128)}, f32[2,512,512]{2,1,0:T(8,128)}, u32[]{:S(2)}, u32[]{:S(2)}) collective-permute-start(f32[2,512,512]{2,1,0:T(8,128)} %get-tuple-element.31), channel_id=1, source_target_pairs={{0,32},{4,36},{8,40},{12,44},{16,48},{20,52},{24,56},{28,60},{32,0... | collective-permute-start | bytes 6291464 | tf_op jit(solution)/shard_map/ppermute | solution.py:12
  318.2 51.3 %collective-permute-start.5 = (f32[2,512,512]{2,1,0:T(8,128)S(1)}, f32[2,512,512]{2,1,0:T(8,128)}, u32[]{:S(2)}, u32[]{:S(2)}) collective-permute-start(f32[2,512,512]{2,1,0:T(8,128)S(1)} %get-tuple-element.16), channel_id=1, source_target_pairs={{0,16},{4,20},{8,24},{12,28},{16,0},{20,4},{24,8},{28,12},{32,48},... | collective-permute-start | bytes 6291464 | tf_op jit(solution)/shard_map/ppermute | solution.py:12
  322.9 88.0 %collective-permute-start.4 = (f32[2,512,512]{2,1,0:T(8,128)}, f32[2,512,512]{2,1,0:T(8,128)}, u32[]{:S(2)}, u32[]{:S(2)}) collective-permute-start(f32[2,512,512]{2,1,0:T(8,128)} %get-tuple-element.17), channel_id=1, source_target_pairs={{0,16},{4,20},{8,24},{12,28},{16,0},{20,4},{24,8},{28,12},{32,48},... | collective-permute-start | bytes 6291464 | tf_op jit(solution)/shard_map/ppermute | solution.py:12
  416.8 49.4 %collective-permute-start.7 = (f32[2,512,512]{2,1,0:T(8,128)}, f32[2,512,512]{2,1,0:T(8,128)S(1)}, u32[]{:S(2)}, u32[]{:S(2)}) collective-permute-start(f32[2,512,512]{2,1,0:T(8,128)} %get-tuple-element.14), channel_id=1, source_target_pairs={{0,8},{4,12},{8,0},{12,4},{16,24},{20,28},{24,16},{28,20},{32,40},... | collective-permute-start | bytes 6291464 | tf_op jit(solution)/shard_map/ppermute | solution.py:12
  419.5 87.6 %collective-permute-start.6 = (f32[2,512,512]{2,1,0:T(8,128)}, f32[2,512,512]{2,1,0:T(8,128)}, u32[]{:S(2)}, u32[]{:S(2)}) collective-permute-start(f32[2,512,512]{2,1,0:T(8,128)} %get-tuple-element.15), channel_id=1, source_target_pairs={{0,8},{4,12},{8,0},{12,4},{16,24},{20,28},{24,16},{28,20},{32,40},... | collective-permute-start | bytes 6291464 | tf_op jit(solution)/shard_map/ppermute | solution.py:12
  466.2 1.3 copy-start.8
  513.2 6.9 collective-permute-start.8
  513.5 7.3 collective-permute-start.9
  567.7 2.8 collective-permute-start.10
  568.0 4.1 collective-permute-start.11
  575.1 26.2 %collective-permute-start.12 = (f32[1,512,512]{2,1,0:T(8,128)}, f32[1,512,512]{2,1,0:T(8,128)S(1)}, u32[]{:S(2)}, u32[]{:S(2)}) collective-permute-start(f32[1,512,512]{2,1,0:T(8,128)} %get-tuple-element.25), channel_id=1, source_target_pairs={{0,8},{4,12},{8,0},{12,4},{16,24},{20,28},{24,16},{28,20},{32,40},... | collective-permute-start | bytes 3145736 | tf_op jit(solution)/shard_map/ppermute | solution.py:12
  576.9 46.3 %collective-permute-start.13 = (f32[1,512,512]{2,1,0:T(8,128)S(1)}, f32[1,512,512]{2,1,0:T(8,128)}, u32[]{:S(2)}, u32[]{:S(2)}) collective-permute-start(f32[1,512,512]{2,1,0:T(8,128)S(1)} %get-tuple-element.24), channel_id=1, source_target_pairs={{0,8},{4,12},{8,0},{12,4},{16,24},{20,28},{24,16},{28,20},{32,40},... | collective-permute-start | bytes 3145736 | tf_op jit(solution)/shard_map/ppermute | solution.py:12
  601.4 1.0 copy-start.11
  625.6 27.7 %copy-start.6 = (f32[1,512,512]{2,1,0:T(8,128)}, f32[1,512,512]{2,1,0:T(8,128)S(1)}, u32[]{:S(2)}) copy-start(f32[1,512,512]{2,1,0:T(8,128)S(1)} %get-tuple-element.22) | copy-start | bytes 3145732
  625.6 27.7 %copy-start.7 = (f32[1,512,512]{2,1,0:T(8,128)}, f32[1,512,512]{2,1,0:T(8,128)S(1)}, u32[]{:S(2)}) copy-start(f32[1,512,512]{2,1,0:T(8,128)S(1)} %get-tuple-element.23) | copy-start | bytes 3145732
  625.6 27.7 %collective-permute-start.14 = (f32[1,512,512]{2,1,0:T(8,128)S(1)}, f32[1,512,512]{2,1,0:T(8,128)S(1)}, u32[]{:S(2)}, u32[]{:S(2)}) collective-permute-start(f32[1,512,512]{2,1,0:T(8,128)S(1)} %get-tuple-element.23), channel_id=1, source_target_pairs={{0,16},{4,20},{8,24},{12,28},{16,0},{20,4},{24,8},{28,12},{32,48},... | collective-permute-start | bytes 3145736 | tf_op jit(solution)/shard_map/ppermute | solution.py:12
  628.7 45.4 %collective-permute-start.15 = (f32[1,512,512]{2,1,0:T(8,128)S(1)}, f32[1,512,512]{2,1,0:T(8,128)}, u32[]{:S(2)}, u32[]{:S(2)}) collective-permute-start(f32[1,512,512]{2,1,0:T(8,128)S(1)} %get-tuple-element.22), channel_id=1, source_target_pairs={{0,16},{4,20},{8,24},{12,28},{16,0},{20,4},{24,8},{28,12},{32,48},... | collective-permute-start | bytes 3145736 | tf_op jit(solution)/shard_map/ppermute | solution.py:12
  676.5 26.2 %collective-permute-start.17 = (f32[1,512,512]{2,1,0:T(8,128)S(1)}, f32[1,512,512]{2,1,0:T(8,128)S(1)}, u32[]{:S(2)}, u32[]{:S(2)}) collective-permute-start(f32[1,512,512]{2,1,0:T(8,128)S(1)} %get-tuple-element.21), channel_id=1, source_target_pairs={{0,32},{4,36},{8,40},{12,44},{16,48},{20,52},{24,56},{28,60},{32,0... | collective-permute-start | bytes 3145736 | tf_op jit(solution)/shard_map/ppermute | solution.py:12
  678.2 44.5 %collective-permute-start.16 = (f32[1,512,512]{2,1,0:T(8,128)S(1)}, f32[1,512,512]{2,1,0:T(8,128)}, u32[]{:S(2)}, u32[]{:S(2)}) collective-permute-start(f32[1,512,512]{2,1,0:T(8,128)S(1)} %get-tuple-element.20), channel_id=1, source_target_pairs={{0,32},{4,36},{8,40},{12,44},{16,48},{20,52},{24,56},{28,60},{32,0... | collective-permute-start | bytes 3145736 | tf_op jit(solution)/shard_map/ppermute | solution.py:12
  678.8 70.1 %copy-start.3 = (f32[512,3,512]{2,0,1:T(8,128)S(1)}, f32[512,3,512]{2,0,1:T(8,128)}, u32[]{:S(2)}) copy-start(f32[512,3,512]{2,0,1:T(8,128)} %copy-done.2) | copy-start | bytes 9437188
  678.8 70.1 %copy-start.13 = (f32[512]{0:T(512)S(1)}, f32[512]{0:T(512)}, u32[]{:S(2)}) copy-start(f32[512]{0:T(512)} %param.9) | copy-start | bytes 6148
  722.6 27.9 %copy-start.1 = (bf16[512,1024]{1,0:T(8,128)(2,1)S(1)}, bf16[512,1024]{1,0:T(8,128)(2,1)}, u32[]{:S(2)}) copy-start(bf16[512,1024]{1,0:T(8,128)(2,1)} %param.5) | copy-start | bytes 3145732
  724.8 24.1 %collective-permute-start.18 = (f32[1,512,512]{2,1,0:T(8,128)S(1)}, f32[1,512,512]{2,1,0:T(8,128)S(1)}, u32[]{:S(2)}, u32[]{:S(2)}) collective-permute-start(f32[1,512,512]{2,1,0:T(8,128)S(1)} %subtract_select_fusion.1), channel_id=1, source_target_pairs={{0,64},{4,68},{8,72},{12,76},{16,80},{20,84},{24,88},{28,92},{32,9... | collective-permute-start | bytes 3145736 | tf_op jit(solution)/shard_map/ppermute | solution.py:12
  (2 other events, 1.9 us)
Sparse Core Ops, SparseCore 0:
  42.8 116.9 reduce-scatter.1
where the time goes:
time: 767 us; the launch traced here: 758 us
  waiting for transfers between devices  589 us (77%)
  matrix products  53.5 us (7%)
  other arithmetic  48.4 us (6%)
  local copies, waits for them, and re-layouts  27.4 us (4%)
  starting transfers between devices  23.9 us (3%)
  between operations  15.4 us (2%)
    ppermute x18, waiting for transfers between devices, swapped(): lax.ppermute(x, axis, [(i, i ^ 1 << bit) for i in range(lax.axis_size(axi...  466 us
    reduce_scatter x1, waiting for transfers between devices, on_device(): lax.psum_scatter(partial_sums.reshape(rows_here, 3, channels_all), 'col',...  117 us
    unnamed x30, local copies, waits for them, and re-layouts  24 us
    ppermute x18, starting transfers between devices, swapped(): lax.ppermute(x, axis, [(i, i ^ 1 << bit) for i in range(lax.axis_size(axi...  23.9 us
    dot_general x1, matrix products, on_device(): jnp.dot(sequence, w_proj.reshape(w_proj.shape[0], 3 * channels_all), pref...  19.4 us
    select_n x3, other arithmetic, forward_butterfly(): imag_part = jnp.where(bottom, turned_imag, imag_part + partner_imag)  18.2 us
    dot_general x4, matrix products, complex_apply(): jnp.einsum(pattern, table_pair[0], stacked, precision=lax.Precision.HIGHEST)  17.2 us
    dot_general x4, matrix products, complex_apply(): jnp.einsum(pattern, table_pair[1], stacked, precision=lax.Precision.HIGHEST)  16.9 us
  transfers between devices with their start and end apart: 20, of which 20 were waited for; matrix products, arithmetic and copies ran while one was open for 0% of the time, Pallas kernels for 0%

commit v1 on v0

v1 whole, which is shorter than its diff:
```python
import numpy as np

import jax
import jax.numpy as jnp
from jax import lax
from jax.sharding import PartitionSpec as P

HIGH = lax.Precision.HIGH


def tables(blocks, rows):
    total = blocks * rows
    outer = np.arange(blocks // 2 + 1)
    inner = np.arange(rows)
    fold = np.arange(blocks)
    a = 2 * np.pi / blocks * (outer[:, None] * fold[None, :] % blocks)
    t = 2 * np.pi / total * (outer[:, None] * inner[None, :] % total)
    f = 2 * np.pi / rows * (inner[:, None] * inner[None, :] % rows)
    both = np.float32
    return [(np.cos(v).astype(both), np.sin(v).astype(both)) for v in (a, t, f)]


def spectrum(x):
    (ac, asn), (tc, ts), (fc, fs) = tables(x.shape[0], x.shape[2])
    re = jnp.einsum("ks,scr->kcr", ac, x, precision=lax.Precision.HIGHEST)
    im = -jnp.einsum("ks,scr->kcr", asn, x, precision=lax.Precision.HIGHEST)
    tc, ts = tc[:, None, :], ts[:, None, :]
    re, im = re * tc + im * ts, im * tc - re * ts
    both = jnp.concatenate([re, im], axis=2)
    turn = np.block([[fc, -fs], [fs, fc]])
    out = jnp.einsum("kcr,rf->kcf", both, turn, precision=HIGH)
    return jnp.split(out, 2, axis=2)


def back(re, im, blocks):
    (ac, asn), (tc, ts), (fc, fs) = tables(blocks, re.shape[2])
    both = jnp.concatenate([re, im], axis=2)
    turn = np.block([[fc, fs], [-fs, fc]])
    re, im = jnp.split(jnp.einsum("kcr,rf->kcf", both, turn, precision=HIGH), 2, axis=2)
    tc, ts = tc[:, None, :], ts[:, None, :]
    re, im = re * tc - im * ts, im * tc + re * ts
    twice = np.full((blocks // 2 + 1, 1), 2.0, np.float32)
    twice[0] = twice[-1] = 1.0
    return jnp.einsum("ks,kcr->scr", ac * twice, re, precision=lax.Precision.HIGHEST) - jnp.einsum(
        "ks,kcr->scr", asn * twice, im, precision=lax.Precision.HIGHEST
    )


def on_device(sequence, w_proj, short_filter, long_filter, skip_gain):
    rows = sequence.shape[0]
    blocks = lax.axis_size("ctx")
    w = w_proj.transpose(1, 0, 2)
    h = lax.all_to_all(long_filter.T.reshape(blocks, -1, rows), "ctx", 0, 0, tiled=False)
    h_re, h_im = spectrum(h)
    partial = jnp.einsum("td,jdc->jtc", sequence, w, preferred_element_type=jnp.float32)
    projected = lax.psum_scatter(partial, "col", scatter_dimension=2, tiled=True)
    size = blocks
    rim = lax.ppermute(projected[:, rows - 2 :], "ctx", [((i - 1) % size, i) for i in range(size)])
    padded = jnp.concatenate([rim, projected], axis=1)
    taps = short_filter[:, :, None, :]
    shaped = taps[0] * projected + taps[1] * padded[:, 1 : rows + 1] + taps[2] * padded[:, 0:rows]
    gated = shaped[1] * shaped[2]
    u = lax.all_to_all(gated.T.reshape(blocks, -1, rows), "ctx", 0, 0, tiled=False)
    re, im = spectrum(u)
    scale = 1.0 / (blocks * rows)
    y_re, y_im = (re * h_re - im * h_im) * scale, (re * h_im + im * h_re) * scale
    y = back(y_re, y_im, blocks)
    conv = lax.all_to_all(y, "ctx", 0, 0, tiled=False).reshape(-1, rows).T
    return shaped[0] * (conv + skip_gain * gated)


def solution(mesh):
    return jax.shard_map(
        on_device,
        mesh=mesh,
        in_specs=(
            P("ctx", "col"),
            P("col", None, None),
            P(None, None, "col"),
            P("ctx", "col"),
            P("col"),
        ),
        out_specs=P("ctx", "col"),
        check_vma=False,
    )
```

time: 767 us -> 230 us (0.30)
  waiting for transfers between devices: 589 us -> 126 us
  other arithmetic: 48.4 us -> 7.96 us
  blocking collectives: 0 us -> 20.8 us
  matrix products: 53.5 us -> 34.1 us
  local copies, waits for them, and re-layouts: 27.4 us -> 12.9 us
  starting transfers between devices: 23.9 us -> 12.4 us
    ppermute x19 -> x1, waiting for transfers between devices: 472 us -> 6.4 us  [on_device(): lax.ppermute(projected[:, rows - 2:], 'ctx', [((i - 1) % size, i) for i i...]
    select_n x9 -> x0, other arithmetic: 32.6 us -> none  [the longest x3 18.2 us: forward_butterfly(): imag_part = jnp.where(bottom, turned_imag, imag_part + partner_imag)]
    ppermute x19 -> x1, starting transfers between devices: 23.9 us -> 0.04 us  [on_device(): lax.ppermute(projected[:, rows - 2:], 'ctx', [((i - 1) % size, i) for i i...]
    all_to_all x0 -> x1, blocking collectives: none -> 20.8 us  [on_device(): conv = lax.all_to_all(y, 'ctx', 0, 0, tiled=False).reshape(-1, rows).T]
    dot_general x9 -> x10, matrix products: 53.5 us -> 34.1 us  [the longest x1 14.5 us: on_device(): jnp.einsum('td,jdc->jtc', sequence, w, preferred_element_type=jnp.float32)]
    unnamed x30 -> x31, local copies, waits for them, and re-layouts: 24 us -> 9.03 us
    all_to_all x0 -> x2, waiting for transfers between devices: none -> 13.6 us  [the longest x1 13.6 us: on_device(): lax.all_to_all(gated.T.reshape(blocks, -1, rows), 'ctx', 0, 0, tiled=False)]
    all_to_all x0 -> x2, starting transfers between devices: none -> 12.4 us  [the longest x1 8.25 us: on_device(): lax.all_to_all(long_filter.T.reshape(blocks, -1, rows), 'ctx', 0, 0, tile...]
  transfers between devices with their start and end apart: 20 -> 4, of which waited for: 20 -> 3; matrix products, arithmetic and copies ran while one was open for 0% -> 6% of each run, Pallas kernels for 0% -> 0%
where the time goes in v1:
time: 230 us; the launch traced here: 228 us
  waiting for transfers between devices  126 us (55%)
  matrix products  34.1 us (15%)
  blocking collectives  20.8 us (9%)
  between operations  13.7 us (6%)
  local copies, waits for them, and re-layouts  12.9 us (6%)
  starting transfers between devices  12.4 us (5%)
  other arithmetic  7.96 us (3%)
    reduce_scatter x1, waiting for transfers between devices, on_device(): lax.psum_scatter(partial, 'col', scatter_dimension=2, tiled=True)  106 us
    all_to_all x1, blocking collectives, on_device(): conv = lax.all_to_all(y, 'ctx', 0, 0, tiled=False).reshape(-1, rows).T  20.8 us
    dot_general x1, matrix products, on_device(): jnp.einsum('td,jdc->jtc', sequence, w, preferred_element_type=jnp.float32)  14.5 us
    all_to_all x1, waiting for transfers between devices, on_device(): lax.all_to_all(gated.T.reshape(blocks, -1, rows), 'ctx', 0, 0, tiled=False)  13.6 us
    unnamed x31, local copies, waits for them, and re-layouts  9.03 us
    all_to_all x1, starting transfers between devices, on_device(): lax.all_to_all(long_filter.T.reshape(blocks, -1, rows), 'ctx', 0, 0, tile...  8.25 us
    ppermute x1, waiting for transfers between devices, on_device(): lax.ppermute(projected[:, rows - 2:], 'ctx', [((i - 1) % size, i) for i i...  6.4 us
    add x1, other arithmetic, on_device(): taps[0] * projected + taps[1] * padded[:, 1:rows + 1]  5.82 us
  transfers between devices with their start and end apart: 4, of which 3 were waited for; matrix products, arithmetic and copies ran while one was open for 6% of the time, Pallas kernels for 0%

profile of v1, /device:TPU:0, one launch (start us, length us, event | category | flops | bytes accessed | tf_op | source)
XLA Modules:
  0.0 228.1 jit_solution(14857614856758406030)
XLA Ops:
  6.5 1.2 copy-done
  7.8 14.5 %fusion.2 = f32[3,512,2048]{1,2,0:T(8,128)} fusion(bf16[1024,3,2048]{2,0,1:T(8,128)(2,1)} %param.21, bf16[512,1024]{1,0:T(8,128)(2,1)S(1)} %copy-done), kind=kOutput, calls=%fused_computation.2 | convolution fusion | flops 6442450944 | bytes 26214400 | tf_op jit(solution)/shard_map/td,jdc->jtc/dot_general | solution.py:55
  22.3 1.2 copy-done.6
  23.5 1.3 copy.45
  24.8 8.2 %all-to-all-start.1 = ((f32[32,16,512]{2,1,0:T(8,128)}), f32[32,16,512]{2,1,0:T(8,128)S(1)}, u32[]{:S(2)}, u32[]{:S(2)}) async-start(f32[32,16,512]{2,1,0:T(8,128)} %bitcast.15), calls=%async_computation.2 | async-start | bytes 2097152 | tf_op jit(solution)/shard_map/all_to_all | solution.py:53
  33.1 106.4 %reduce-scatter.2.cloned.1.call-done = f32[3,512,512]{1,2,0:T(8,128)} async-done(((f32[3,512,2048]{1,2,0:T(8,128)}), f32[3,512,512]{1,2,0:T(8,128)}) %reduce-scatter.2.cloned.1.call-update) | async-done | bytes 3145744 | tf_op jit(solution)/shard_map/reduce_scatter | solution.py:56
  139.5 1.4 slice.39
  140.9 0.3 copy.40
  141.2 6.4 %collective-permute-done = f32[3,2,512]{2,1,0:T(2,128)S(1)} collective-permute-done((f32[3,2,512]{2,1,0:T(2,128)S(1)}, f32[3,2,512]{2,1,0:T(2,128)S(1)}, u32[]{:S(2)}, u32[]{:S(2)}) %collective-permute-start) | collective-permute-done | bytes 12320 | tf_op jit(solution)/shard_map/ppermute | solution.py:58
  147.6 0.3 copy.41
  147.9 5.8 %fusion.8 = f32[3,512,512]{1,2,0:T(8,128)S(1)} fusion(f32[3,2,512]{1,2,0:T(8,128)S(1)} %copy.41, f32[3,512,512]{1,2,0:T(8,128)} %reduce-scatter.2.cloned.1.call-done, f32[3,512]{1,0:T(4,128)S(1)} %get-tuple-element.14, f32[3,512]{1,0:T(4,128)S(1)} %get-tuple-element.15, f32[3,512]{1,0:T(4,128)S(1)} %get-tuple-element.13), kind=kLoop, calls=%fused_computation.8 | loop fusion | flops 5505024 | bytes 6322176 | tf_op jit(solution)/shard_map/add | solution.py:61
  153.7 1.6 copy-done.2
  155.4 1.2 slice_multiply_fusion
  156.6 4.1 %all-to-all-start = ((f32[32,16,512]{2,1,0:T(8,128)}), f32[32,16,512]{2,1,0:T(8,128)S(1)}, u32[]{:S(2)}, u32[]{:S(2)}) async-start(f32[32,16,512]{2,1,0:T(8,128)} %bitcast.10), calls=%async_computation.1 | async-start | bytes 2097152 | tf_op jit(solution)/shard_map/all_to_all | solution.py:63
  160.7 1.3 fusion.21
  162.1 2.2 convolution_negate_fusion
  164.3 13.6 %all-to-all-done = f32[32,16,512]{2,1,0:T(8,128)S(1)} async-done(((f32[32,16,512]{2,1,0:T(8,128)}), f32[32,16,512]{2,1,0:T(8,128)S(1)}, u32[]{:S(2)}, u32[]{:S(2)}) %all-to-all-start) | async-done | bytes 1048608 | tf_op jit(solution)/shard_map/all_to_all | solution.py:63
  177.8 1.3 fusion.24
  179.2 3.0 %multiply_add_fusion.1 = (f32[17,16,512]{2,0,1:T(8,128)S(1)}, f32[17,16,512]{2,0,1:T(8,128)S(1)}, f32[17,16,512]{2,0,1:T(8,128)S(1)}, f32[17,16,512]{2,0,1:T(8,128)S(1)}) fusion(f32[17,16,512]{2,0,1:T(8,128)S(1)} %fusion.24, f32[17,512]{1,0:T(8,128)S(1)} %copy-done.7, f32[17,512]{1,0:T(8,128)S(1)} %copy-done.8, f32[17,16,512]{2,0,1:T(8,128)S(1)} %fusion.21, ...), kind=kOutput, calls=%fused_computation.47 | convolution fusion | flops 55287808 | bytes 5019776 | tf_op jit(solution)/shard_map/ks,scr->kcr/dot_general | solution.py:26
  182.2 0.4 pad_maximum_fusion.1
  182.6 1.8 copy-done.4
  184.4 2.8 %fusion.14 = f32[17,16,1024]{2,1,0:T(8,128)S(1)} fusion(f32[1024,1024,1]{1,0,2:T(8,128)S(1)} %copy-done.4, f32[17,16,1024]{2,0,1:T(8,128)S(1)} %get-tuple-element.17), kind=kOutput, calls=%fused_computation.21 | convolution fusion | flops 1711276032 | bytes 6422528 | tf_op jit(solution)/shard_map/kcr,rf->kcf/dot_general | solution.py:31
  187.2 2.8 %fusion.16 = f32[17,16,1024]{2,1,0:T(8,128)S(1)} fusion(f32[1024,1024,1]{1,0,2:T(8,128)S(1)} %copy-done.4, f32[17,16,1024]{2,0,1:T(8,128)S(1)} %get-tuple-element.16), kind=kOutput, calls=%fused_computation.23 | convolution fusion | flops 1711276032 | bytes 6422528 | tf_op jit(solution)/shard_map/kcr,rf->kcf/dot_general | solution.py:31
  190.1 0.3 subtract_multiply_fusion
  190.4 1.8 copy-done.5
  192.2 3.6 %fusion.10 = f32[17,16,1024]{2,0,1:T(8,128)S(1)} fusion(f32[1024,1024,1]{1,0,2:T(8,128)S(1)} %copy-done.5, f32[17,16,1024]{2,1,0:T(8,128)S(1)} %pad_maximum_fusion.3), kind=kOutput, calls=%fused_computation.13 | convolution fusion | flops 1711276032 | bytes 6422528 | tf_op jit(solution)/shard_map/kcr,rf->kcf/dot_general | solution.py:39
  195.9 1.2 fusion.29
  197.1 1.2 fusion.12
  198.3 0.6 copy.51
  198.9 20.8 %all_to_all.15 = f32[32,16,512]{2,1,0:T(8,128)S(1)} all-to-all(f32[32,16,512]{2,1,0:T(8,128)S(1)} %copy.51), channel_id=1, replica_groups=mesh['ctx'=32,'col'=4] {'ctx'}, dimensions={0} | all-to-all | bytes 2097152 | tf_op jit(solution)/shard_map/all_to_all | solution.py:68
  219.7 0.2 fusion.18
  220.0 1.3 copy.52
  (31 shorter events, 0.2 us)
Async XLA Ops:
  6.5 1.2 copy-start
  6.5 132.9 %reduce-scatter.2.cloned.1.call-start = ((), (), s32[]{:S(2)}) async-start(), calls=%async_computation.4 | async-start | bytes 15728640 | tf_op jit(solution)/shard_map/reduce_scatter | solution.py:56
  22.3 1.2 copy-start.6
  23.5 117.7 %copy-start.11 = (f32[3,3,512]{2,1,0:T(4,128)S(1)}, f32[3,3,512]{2,1,0:T(4,128)}, u32[]{:S(2)}) copy-start(f32[3,3,512]{2,1,0:T(4,128)} %param.22) | copy-start | bytes 55300
  24.8 131.7 %all-to-all-start.1 = ((f32[32,16,512]{2,1,0:T(8,128)}), f32[32,16,512]{2,1,0:T(8,128)S(1)}, u32[]{:S(2)}, u32[]{:S(2)}) async-start(f32[32,16,512]{2,1,0:T(8,128)} %bitcast.15), calls=%async_computation.2 | async-start | bytes 2097152 | tf_op jit(solution)/shard_map/all_to_all | solution.py:53
  141.1 6.5 %collective-permute-start = (f32[3,2,512]{2,1,0:T(2,128)S(1)}, f32[3,2,512]{2,1,0:T(2,128)S(1)}, u32[]{:S(2)}, u32[]{:S(2)}) collective-permute-start(f32[3,2,512]{2,1,0:T(2,128)S(1)} %copy.40), channel_id=1, source_target_pairs={{124,0},{0,4},{4,8},{8,12},{12,16},{16,20},{20,24},{24,28},{28,32}... | collective-permute-start | bytes 36872 | tf_op jit(solution)/shard_map/ppermute | solution.py:58
  153.7 1.6 copy-start.2
  155.4 5.3 %copy-start.9 = (f32[17,32,1]{1,0,2:T(8,128)S(1)}, f32[17,32,1]{1,0,2:T(8,128)}, u32[]{:S(2)}) copy-start(f32[17,32,1]{1,0,2:T(8,128)} %constant.28) | copy-start | bytes 6532
  155.4 6.7 %copy-start.10 = (f32[17,32,1]{1,0,2:T(8,128)S(1)}, f32[17,32,1]{1,0,2:T(8,128)}, u32[]{:S(2)}) copy-start(f32[17,32,1]{1,0,2:T(8,128)} %constant.29) | copy-start | bytes 6532
  156.6 21.3 %all-to-all-start = ((f32[32,16,512]{2,1,0:T(8,128)}), f32[32,16,512]{2,1,0:T(8,128)S(1)}, u32[]{:S(2)}, u32[]{:S(2)}) async-start(f32[32,16,512]{2,1,0:T(8,128)} %bitcast.10), calls=%async_computation.1 | async-start | bytes 2097152 | tf_op jit(solution)/shard_map/all_to_all | solution.py:63
  160.7 18.5 %copy-start.7 = (f32[17,512]{1,0:T(8,128)S(1)}, f32[17,512]{1,0:T(8,128)}, u32[]{:S(2)}) copy-start(f32[17,512]{1,0:T(8,128)} %constant.27) | copy-start | bytes 104452
  160.7 18.5 %copy-start.8 = (f32[17,512]{1,0:T(8,128)S(1)}, f32[17,512]{1,0:T(8,128)}, u32[]{:S(2)}) copy-start(f32[17,512]{1,0:T(8,128)} %constant.26) | copy-start | bytes 104452
  182.2 2.2 copy-start.4
  190.0 2.2 copy-start.5
  192.2 3.6 %copy-start.13 = (f32[17,32,1]{1,0,2:T(8,128)S(1)}, f32[17,32,1]{1,0,2:T(8,128)}, u32[]{:S(2)}) copy-start(f32[17,32,1]{1,0,2:T(8,128)} %constant.32) | copy-start | bytes 6532
  192.2 4.8 %copy-start.12 = (f32[17,32,1]{1,0,2:T(8,128)S(1)}, f32[17,32,1]{1,0,2:T(8,128)}, u32[]{:S(2)}) copy-start(f32[17,32,1]{1,0,2:T(8,128)} %constant.33) | copy-start | bytes 6532
  197.1 22.7 %copy-start.3 = (f32[3,512,512]{1,2,0:T(8,128)S(1)}, f32[3,512,512]{1,2,0:T(8,128)}, u32[]{:S(2)}) copy-start(f32[3,512,512]{1,2,0:T(8,128)} %copy-done.2) | copy-start | bytes 9437188
  197.1 22.7 %copy-start.14 = (f32[512]{0:T(512)S(1)}, f32[512]{0:T(512)}, u32[]{:S(2)}) copy-start(f32[512]{0:T(512)} %param.24) | copy-start | bytes 6148
  198.9 22.4 %copy-start.1 = (bf16[512,1024]{1,0:T(8,128)(2,1)S(1)}, bf16[512,1024]{1,0:T(8,128)(2,1)}, u32[]{:S(2)}) copy-start(bf16[512,1024]{1,0:T(8,128)(2,1)} %param.20) | copy-start | bytes 3145732
Sparse Core Ops, SparseCore 0:
  22.5 116.9 reduce-scatter.1

commit v2 on v1

v2 whole, which is shorter than its diff:
```python
import functools

import ml_dtypes
import numpy as np

import jax
import jax.numpy as jnp
from jax import lax
from jax.experimental import pallas as pl
from jax.experimental.pallas import tpu as pltpu
from jax.sharding import PartitionSpec as P

MESH = pl.DeviceIdType.MESH
F32 = jnp.float32
BF16 = jnp.bfloat16
LANES = 128
RIM = 8

TILES = ((1, 0), (2, 0), (1, 1), (2, 1), (0, 0), (0, 1))


def tables(blocks, rows):
    outer, inner = np.arange(blocks // 2 + 1), np.arange(rows)
    turn = 2 * np.pi / (blocks * rows) * (outer[:, None] * inner[None, :] % (blocks * rows))
    angle = 2 * np.pi / rows * (inner[:, None] * inner[None, :] % rows)
    result = []
    for full in (np.cos(angle), np.sin(angle)):
        high = full.astype(ml_dtypes.bfloat16)
        result += [high, (full - high.astype(np.float64)).astype(ml_dtypes.bfloat16)]
    return result + [np.cos(turn).astype(np.float32), np.sin(turn).astype(np.float32)]


def scaled(value, factor):
    return value if factor == 1.0 else value * factor


def turned(value, k, n, sign):
    re, im = value
    c, s = float(np.cos(2 * np.pi * k / n)), sign * float(np.sin(2 * np.pi * k / n))
    if k == 0:
        return value
    if 4 * k == n:
        return (None if im is None else im * -s, re * s)
    if im is None:
        return (re * c, re * s)
    return (re * c - im * s, re * s + im * c)


def plus(a, b):
    return a if b is None else b if a is None else a + b


def minus(a, b):
    return a if b is None else -b if a is None else a - b


def real_dft(x):
    n = len(x)
    if n == 1:
        return [(x[0], None)]
    if n == 2:
        return [(x[0] + x[1], None), (x[0] - x[1], None)]
    even, odd = real_dft(x[0::2]), real_dft(x[1::2])
    result = [None] * (n // 2 + 1)
    for k in range(n // 4 + 1):
        (er, ei), (orr, oi) = even[k], turned(odd[k], k, n, -1.0)
        result[k] = (plus(er, orr), plus(ei, oi))
        if 2 * k != n // 2:
            result[n // 2 - k] = (minus(er, orr), minus(oi, ei) if ei is not None or oi is not None else None)
    return result


def real_inverse(f, n):
    if n == 2:
        return [f[0][0] + f[1][0], f[0][0] - f[1][0]]
    even, odd = [], []
    for k in range(n // 4 + 1):
        (ar, ai), (br, bi) = f[k], f[n // 2 - k]
        if 2 * k == n // 2:
            even.append((ar + ar, None))
            odd.append((None if ai is None else -2.0 * ai, None))
            continue
        even.append((ar + br, None if k == 0 else minus(ai, bi)))
        odd.append(turned((ar - br, None if k == 0 else plus(ai, bi)), k, n, 1.0))
    result = [None] * n
    result[0::2] = real_inverse(even, n // 2)
    result[1::2] = real_inverse(odd, n // 2)
    return result


def split(value):
    high = value.astype(BF16)
    return high, (value - high.astype(F32)).astype(BF16)


def kernel(
    blocks,
    x_ref,
    w_hbm,
    taps_ref,
    h_ref,
    gain_ref,
    table_hbm,
    turn_ref,
    out_ref,
    w_vm,
    table,
    part,
    relay,
    from_sum,
    from_one,
    fin,
    h_sent,
    h_got,
    u_kept,
    u_sent,
    u_got,
    y_sent,
    y_got,
    h_freq,
    work,
    w_sem,
    table_sem,
    tile_send,
    tile_recv,
    rim_send,
    rim_recv,
    swap_send,
    swap_recv,
):
    me, row = lax.axis_index("ctx"), lax.axis_index("col")
    rows, wide = x_ref.shape[0], part.shape[3]
    per = wide // blocks
    freqs = blocks // 2 + 1
    half = freqs * per
    tiles = len(TILES)
    peers = blocks - 1

    def at_col(offset):
        return (me, lax.rem(row + offset, 4))

    def peer(i):
        return lax.rem(me + i, blocks)

    def weight_copy(t, o):
        j, g = TILES[t]
        start = pl.multiple_of(lax.rem(row + o, 4) * (2 * wide) + g * wide, LANES)
        return pltpu.make_async_copy(w_hbm.at[j, :, pl.ds(start, wide)], w_vm.at[t, o], w_sem.at[t, o])

    barrier = pltpu.get_barrier_semaphore()

    @pl.loop(1, blocks)
    def _(i):
        pl.semaphore_signal(barrier, inc=1, device_id=(peer(i), row), device_id_type=MESH)

    for offset in (1, 3):
        pl.semaphore_signal(barrier, inc=1, device_id=at_col(offset), device_id_type=MESH)

    for pair in range(tiles // 2):
        for order in ((2, 2), (3, 1), (1, 3), (0, 0)):
            for s in range(2):
                weight_copy(2 * pair + s, order[s]).start()
    table_copy = pltpu.make_async_copy(table_hbm, table, table_sem)
    table_copy.start()

    def project(t, o):
        pltpu.make_async_copy(w_vm.at[t, o], w_vm.at[t, o], w_sem.at[t, o]).wait()
        part[t, o] = jnp.dot(x_ref[...], w_vm[t, o], preferred_element_type=F32)

    def tile_copy(t, s, kind):
        onward, backward = 1 + 2 * s, 3 - 2 * s
        place, target, offset = (
            (2, relay, onward),
            (onward, from_sum, onward),
            (backward, from_one, backward),
        )[kind]
        return pltpu.make_async_remote_copy(
            src_ref=part.at[t, place],
            dst_ref=target.at[t],
            send_sem=tile_send.at[kind, t],
            recv_sem=tile_recv.at[kind, t],
            device_id=at_col(offset),
            device_id_type=MESH,
        )

    def send_far(pair):
        @pl.loop(0, 2)
        def _(s):
            project(2 * pair + s, 2)
            tile_copy(2 * pair + s, s, 0).start()

    def send_one(pair):
        @pl.loop(0, 2)
        def _(s):
            project(2 * pair + s, 3 - 2 * s)
            tile_copy(2 * pair + s, s, 2).start()

    def project_rest(pair):
        @pl.loop(0, 2)
        def _(s):
            project(2 * pair + s, 1 + 2 * s)
            project(2 * pair + s, 0)

    def send_sum(pair):
        @pl.loop(0, 2)
        def _(s):
            t = 2 * pair + s
            tile_copy(t, s, 0).wait_recv()

            @pl.loop(0, rows // LANES)
            def _(r):
                at = pl.ds(pl.multiple_of(r * LANES, LANES), LANES)
                part[t, 1 + 2 * s, at] = part[t, 1 + 2 * s, at] + relay[t, at]

            tile_copy(t, s, 1).start()

    def rim_copy(t):
        return pltpu.make_async_remote_copy(
            src_ref=fin.at[t, pl.ds(rows, RIM)],
            dst_ref=fin.at[t, pl.ds(0, RIM)],
            send_sem=rim_send.at[t],
            recv_sem=rim_recv.at[t],
            device_id=(peer(1), row),
            device_id_type=MESH,
        )

    def finish(pair):
        @pl.loop(0, 2)
        def _(s):
            t = 2 * pair + s
            tile_copy(t, s, 2).wait_recv()
            tile_copy(t, s, 1).wait_recv()
            last = pl.ds(rows - RIM, RIM)
            fin[t, pl.ds(rows, RIM)] = part[t, 0, last] + from_sum[t, last] + from_one[t, last]
            rim_copy(t).start()

            @pl.loop(0, rows // LANES - 1)
            def _(r):
                at = pl.ds(pl.multiple_of(r * LANES, LANES), LANES)
                to = pl.ds(pl.multiple_of(r * LANES + RIM, RIM), LANES)
                fin[t, to] = part[t, 0, at] + from_sum[t, at] + from_one[t, at]

            at = pl.ds(rows - LANES, LANES - RIM)
            fin[t, pl.ds(rows - LANES + RIM, LANES - RIM)] = part[t, 0, at] + from_sum[t, at] + from_one[t, at]

        @pl.loop(0, 2)
        def _(s):
            rim_copy(2 * pair + s).wait_recv()

    def shaped(t, r):
        j, g = TILES[t]
        near = fin[t, pl.ds(pl.multiple_of(r * LANES, LANES), LANES + RIM)]
        tap = [taps_ref[i, j : j + 1, g * wide : (g + 1) * wide] for i in range(3)]
        return (
            tap[0] * near[RIM:] + tap[1] * near[RIM - 1 : RIM - 1 + LANES] + tap[2] * near[RIM - 2 : RIM - 2 + LANES]
        )

    def swap_start(which, g, source, target):
        @pl.loop(1, blocks)
        def _(i):
            p = peer(i)
            if which == 2:
                src, dst = source.at[g, p], target.at[g, pl.ds(pl.multiple_of(me * per, per), per)]
            else:
                src, dst = source.at[g, pl.ds(pl.multiple_of(p * per, per), per)], target.at[g, me]
            pltpu.make_async_remote_copy(
                src_ref=src,
                dst_ref=dst,
                send_sem=swap_send.at[which, g],
                recv_sem=swap_recv.at[which, g],
                device_id=(p, row),
                device_id_type=MESH,
            ).start()

        own = pl.ds(pl.multiple_of(me * per, per), per)
        if which == 2:
            target[g, own] = source[g, me]
        else:
            target[g, me] = source[g, own]

    def swap_wait(sem, which, g):
        held = h_got.at[0, pl.ds(0, peers)]
        pltpu.make_async_copy(held, held, sem.at[which, g]).wait()

    def times_tables(value):
        high, low = split(value)
        result = []
        for i in (0, 2):
            both = jnp.dot(jnp.concatenate([high, low], axis=0), table[i], preferred_element_type=F32)
            result.append(both[: 2 * half] + both[2 * half :] + jnp.dot(high, table[i + 1], preferred_element_type=F32))
        return result

    def spectrum(source, g):
        @pl.loop(0, rows // LANES)
        def _(r):
            at = pl.ds(pl.multiple_of(r * LANES, LANES), LANES)
            found = real_dft([source[g, s, :, at] for s in range(blocks)])
            for k, (re, im) in enumerate(found):
                c, s = turn_ref[0, k : k + 1, at], turn_ref[1, k : k + 1, at]
                work[k * per : (k + 1) * per, at] = re * c if im is None else re * c + im * s
                work[half + k * per : half + (k + 1) * per, at] = -re * s if im is None else im * c - re * s

        by_cos, by_sin = times_tables(work[...])
        return by_cos[:half] + by_sin[half:], by_cos[half:] - by_sin[:half]

    def convolve(g):
        re, im = spectrum(u_got, g)
        h_re, h_im = h_freq[g, :half], h_freq[g, half:]
        product = jnp.concatenate([re * h_re - im * h_im, re * h_im + im * h_re], axis=0)
        by_cos, by_sin = times_tables(product)
        work[:half] = by_cos[:half] - by_sin[half:]
        work[half:] = by_cos[half:] + by_sin[:half]

        @pl.loop(0, rows // LANES)
        def _(r):
            at = pl.ds(pl.multiple_of(r * LANES, LANES), LANES)
            freq = []
            for k in range(freqs):
                c, s = turn_ref[0, k : k + 1, at], turn_ref[1, k : k + 1, at]
                re, im = work[k * per : (k + 1) * per, at], work[half + k * per : half + (k + 1) * per, at]
                freq.append((re * c - im * s, None if k in (0, freqs - 1) else re * s + im * c))
            for s, value in enumerate(real_inverse(freq, blocks)):
                y_sent[g, s, :, at] = value

    def gate(g):
        for r in range(rows // LANES):
            at = slice(r * LANES, (r + 1) * LANES)
            u = shaped(2 * g, r) * shaped(2 * g + 1, r)
            u_kept[g, at] = u
            u_sent[g, :, at] = u.T
        swap_start(1, g, u_sent, u_got)

    def through(g):
        swap_wait(swap_recv, 1, g)
        convolve(g)
        swap_start(2, g, y_sent, y_got)

    pl.semaphore_wait(barrier, peers + 2)
    send_far(0)
    send_one(0)
    for g in range(2):
        for r in range(rows // LANES):
            at = slice(r * LANES, (r + 1) * LANES)
            h_sent[g, :, at] = h_ref[at, g * wide : (g + 1) * wide].T
        swap_start(0, g, h_sent, h_got)
    project_rest(0)
    send_sum(0)
    send_far(1)
    send_one(1)
    project_rest(1)
    table_copy.wait()
    scale = 1.0 / (blocks * rows)
    for g in range(2):
        swap_wait(swap_recv, 0, g)

    @pl.loop(0, 2)
    def _(g):
        re, im = spectrum(h_got, g)
        h_freq[g, :half] = re * scale
        h_freq[g, half:] = im * scale

    finish(0)
    gate(0)
    send_sum(1)
    send_far(2)
    send_one(2)
    project_rest(2)
    through(0)
    finish(1)
    gate(1)
    through(1)
    send_sum(2)
    finish(2)
    for g in range(2):
        swap_wait(swap_recv, 2, g)
        for r in range(rows // LANES):
            at = slice(r * LANES, (r + 1) * LANES)
            gain = gain_ref[:, g * wide : (g + 1) * wide]
            out_ref[at, g * wide : (g + 1) * wide] = shaped(4 + g, r) * (y_got[g, :, at].T + gain * u_kept[g, at])

    @pl.loop(0, tiles // 2)
    def _(pair):
        @pl.loop(0, 2)
        def _(s):
            t = 2 * pair + s
            rim_copy(t).wait_send()
            for kind in range(3):
                tile_copy(t, s, kind).wait_send()

    for which in range(3):
        for g in range(2):
            swap_wait(swap_send, which, g)


def on_device(blocks, sequence, w_proj, short_filter, long_filter, skip_gain):
    rows, depth = sequence.shape
    channels = long_filter.shape[1]
    wide = channels // 2
    per = wide // blocks
    freqs = blocks // 2 + 1
    tiles = len(TILES)
    *turn_tables, turn_cos, turn_sin = tables(blocks, rows)
    vmem = pl.BlockSpec(memory_space=pltpu.VMEM)
    hbm = pl.BlockSpec(memory_space=pl.ANY)
    tile = (tiles, rows, wide)
    sharded = (2, blocks, per, rows)
    flipped = (2, wide, rows)
    return pl.pallas_call(
        functools.partial(kernel, blocks),
        out_shape=jax.ShapeDtypeStruct((rows, channels), F32),
        in_specs=[vmem, hbm, vmem, vmem, vmem, hbm, vmem],
        out_specs=vmem,
        scratch_shapes=[
            pltpu.VMEM((tiles, 4, depth, wide), BF16),
            pltpu.VMEM((4, rows, rows), BF16),
            pltpu.VMEM((tiles, 4, rows, wide), F32),
            pltpu.VMEM(tile, F32),
            pltpu.VMEM(tile, F32),
            pltpu.VMEM(tile, F32),
            pltpu.VMEM((tiles, rows + RIM, wide), F32),
            pltpu.VMEM(flipped, F32),
            pltpu.VMEM(sharded, F32),
            pltpu.VMEM((2, rows, wide), F32),
            pltpu.VMEM(flipped, F32),
            pltpu.VMEM(sharded, F32),
            pltpu.VMEM(sharded, F32),
            pltpu.VMEM(flipped, F32),
            pltpu.VMEM((2, 2 * freqs * per, rows), F32),
            pltpu.VMEM((2 * freqs * per, rows), F32),
            pltpu.SemaphoreType.DMA((tiles, 4)),
            pltpu.SemaphoreType.DMA,
            pltpu.SemaphoreType.DMA((3, tiles)),
            pltpu.SemaphoreType.DMA((3, tiles)),
            pltpu.SemaphoreType.DMA((tiles,)),
            pltpu.SemaphoreType.DMA((tiles,)),
            pltpu.SemaphoreType.DMA((3, 2)),
            pltpu.SemaphoreType.DMA((3, 2)),
        ],
        compiler_params=pltpu.CompilerParams(
            collective_id=0, has_side_effects=True, vmem_limit_bytes=60 << 20
        ),
        cost_estimate=pl.CostEstimate(
            flops=2 * rows * depth * 12 * channels, bytes_accessed=16 << 20, transcendentals=0
        ),
    )(
        sequence,
        w_proj.transpose(1, 0, 2),
        short_filter,
        long_filter,
        skip_gain[None, :],
        np.stack(turn_tables),
        np.stack([turn_cos, turn_sin]),
    )


def solution(mesh):
    return jax.shard_map(
        functools.partial(on_device, mesh.shape["ctx"]),
        mesh=mesh,
        in_specs=(
            P("ctx", "col"),
            P("col", None, None),
            P(None, None, "col"),
            P("ctx", "col"),
            P("col"),
        ),
        out_specs=P("ctx", "col"),
        check_vma=False,
    )
```

time: 230 us -> 121 us (0.53)
  waiting for transfers between devices: 126 us -> 0 us
  Pallas kernels: 0 us -> 118 us
  matrix products: 34.1 us -> 0 us
  blocking collectives: 20.8 us -> 0 us
  between operations: 13.7 us -> 0.01 us
  starting transfers between devices: 12.4 us -> 0 us
  local copies, waits for them, and re-layouts: 12.9 us -> 2.26 us
  other arithmetic: 7.96 us -> 0 us
    pallas_call x0 -> x1, Pallas kernels: none -> 118 us  [on_device(): pl.pallas_call(functools.partial(kernel, blocks), out_shape=jax.ShapeDtyp...]
    reduce_scatter x1 -> x0, waiting for transfers between devices: 106 us -> none  [on_device(): lax.psum_scatter(partial, 'col', scatter_dimension=2, tiled=True)]
    dot_general x10 -> x0, matrix products: 34.1 us -> none  [the longest x1 14.5 us: on_device(): jnp.einsum('td,jdc->jtc', sequence, w, preferred_element_type=jnp.float32)]
    all_to_all x1 -> x0, blocking collectives: 20.8 us -> none  [on_device(): conv = lax.all_to_all(y, 'ctx', 0, 0, tiled=False).reshape(-1, rows).T]
    all_to_all x2 -> x0, waiting for transfers between devices: 13.6 us -> none  [the longest x1 13.6 us: on_device(): lax.all_to_all(gated.T.reshape(blocks, -1, rows), 'ctx', 0, 0, tiled=False)]
    all_to_all x2 -> x0, starting transfers between devices: 12.4 us -> none  [the longest x1 8.25 us: on_device(): lax.all_to_all(long_filter.T.reshape(blocks, -1, rows), 'ctx', 0, 0, tile...]
    unnamed x31 -> x1, local copies, waits for them, and re-layouts: 9.03 us -> 2.26 us
    ppermute x1 -> x0, waiting for transfers between devices: 6.4 us -> none  [on_device(): lax.ppermute(projected[:, rows - 2:], 'ctx', [((i - 1) % size, i) for i i...]
  transfers between devices with their start and end apart: 4 -> 0, of which waited for: 3 -> 0; matrix products, arithmetic and copies ran while one was open for 6% -> 0% of each run, Pallas kernels for 0% -> 0%
where the time goes in v2:
time: 121 us; the launch traced here: 120 us
  Pallas kernels  118 us (98%)
  local copies, waits for them, and re-layouts  2.26 us (2%)
    pallas_call x1, Pallas kernels, on_device(): pl.pallas_call(functools.partial(kernel, blocks), out_shape=jax.ShapeDtyp...  118 us

profile of v2, /device:TPU:0, one launch (start us, length us, event | category | flops | bytes accessed | tf_op | source)
XLA Modules:
  0.0 120.1 jit_solution(2795794650279575633)
XLA Ops:
  0.0 117.9 %shard_map.73 = f32[512,512]{1,0:T(8,128)} custom-call(bf16[512,1024]{1,0:T(8,128)(2,1)} %x_ref.1, bf16[3,1024,2048]{2,1,0:T(8,128)(2,1)} %bitcast.2, f32[3,3,512]{2,1,0:T(4,128)} %taps_ref.1, f32[512,512]{1,0:T(8,128)} %h_ref.1, f32[1,512]{1,0:T(1,128)} %bitcast.3, bf16[4,512,512]{2,1,0:T(8,128)(2,1)} %constant.4.clone.table_hbm, ...), custom_call_target="tpu_custom_call" | custom-call | flops 6442450944 | bytes 16777216 | tf_op jit(solution)/shard_map/pallas_call | solution.py:408
  117.9 2.3 %copy.9 = f32[512,512]{1,0:T(8,128)} copy(f32[512,512]{1,0:T(8,128)} %shard_map.73) | data formatting | bytes 2097152

commit v3 on v2

--- a/solution.py
+++ b/solution.py
@@ -95,13 +95,16 @@
 
 def kernel(
     blocks,
-    x_ref,
+    x_hbm,
     w_hbm,
     taps_ref,
-    h_ref,
+    h_hbm,
     gain_ref,
     table_hbm,
     turn_ref,
+    out_hbm,
+    x_ref,
+    h_ref,
     out_ref,
     w_vm,
     table,
@@ -120,7 +123,10 @@
     h_freq,
     work,
     w_sem,
-    table_sem,
+    side_sem,
+    out_sem,
+    sum_send,
+    sum_recv,
     tile_send,
     tile_recv,
     rim_send,
@@ -130,6 +136,7 @@
 ):
     me, row = lax.axis_index("ctx"), lax.axis_index("col")
     rows, wide = x_ref.shape[0], part.shape[3]
+    chunks = rows // LANES
     per = wide // blocks
     freqs = blocks // 2 + 1
     half = freqs * per
@@ -156,11 +163,16 @@
     for offset in (1, 3):
         pl.semaphore_signal(barrier, inc=1, device_id=at_col(offset), device_id_type=MESH)
 
+    x_copy = pltpu.make_async_copy(x_hbm, x_ref, side_sem.at[0])
+    h_copy = pltpu.make_async_copy(h_hbm, h_ref, side_sem.at[1])
+    table_copy = pltpu.make_async_copy(table_hbm, table, side_sem.at[2])
+    x_copy.start()
     for pair in range(tiles // 2):
         for order in ((2, 2), (3, 1), (1, 3), (0, 0)):
             for s in range(2):
                 weight_copy(2 * pair + s, order[s]).start()
-    table_copy = pltpu.make_async_copy(table_hbm, table, table_sem)
+        if pair == 0:
+            h_copy.start()
     table_copy.start()
 
     def project(t, o):
@@ -169,11 +181,7 @@
 
     def tile_copy(t, s, kind):
         onward, backward = 1 + 2 * s, 3 - 2 * s
-        place, target, offset = (
-            (2, relay, onward),
-            (onward, from_sum, onward),
-            (backward, from_one, backward),
-        )[kind]
+        place, target, offset = ((2, relay, onward), (backward, from_one, backward))[kind]
         return pltpu.make_async_remote_copy(
             src_ref=part.at[t, place],
             dst_ref=target.at[t],
@@ -183,17 +191,34 @@
             device_id_type=MESH,
         )
 
+    def sum_copy(t, s, r):
+        at = pl.ds(pl.multiple_of(r * LANES, LANES), LANES)
+        return pltpu.make_async_remote_copy(
+            src_ref=part.at[t, 1 + 2 * s, at],
+            dst_ref=from_sum.at[t, at],
+            send_sem=sum_send.at[t, r],
+            recv_sem=sum_recv.at[t, r],
+            device_id=at_col(1 + 2 * s),
+            device_id_type=MESH,
+        )
+
     def send_far(pair):
         @pl.loop(0, 2)
         def _(s):
             project(2 * pair + s, 2)
+            if pair == 0:
+
+                @pl.when(s == 0)
+                def _():
+                    pl.semaphore_wait(barrier, peers + 2)
+
             tile_copy(2 * pair + s, s, 0).start()
 
     def send_one(pair):
         @pl.loop(0, 2)
         def _(s):
             project(2 * pair + s, 3 - 2 * s)
-            tile_copy(2 * pair + s, s, 2).start()
+            tile_copy(2 * pair + s, s, 1).start()
 
     def project_rest(pair):
         @pl.loop(0, 2)
@@ -204,15 +229,18 @@
     def send_sum(pair):
         @pl.loop(0, 2)
         def _(s):
-            t = 2 * pair + s
-            tile_copy(t, s, 0).wait_recv()
-
-            @pl.loop(0, rows // LANES)
-            def _(r):
+            tile_copy(2 * pair + s, s, 0).wait_recv()
+
+        @pl.loop(0, chunks)
+        def _(i):
+            r = chunks - 1 - i
+
+            @pl.loop(0, 2)
+            def _(s):
+                t = 2 * pair + s
                 at = pl.ds(pl.multiple_of(r * LANES, LANES), LANES)
                 part[t, 1 + 2 * s, at] = part[t, 1 + 2 * s, at] + relay[t, at]
-
-            tile_copy(t, s, 1).start()
+                sum_copy(t, s, r).start()
 
     def rim_copy(t):
         return pltpu.make_async_remote_copy(
@@ -224,28 +252,39 @@
             device_id_type=MESH,
         )
 
+    def finish_chunk(pair, r):
+        @pl.loop(0, 2)
+        def _(s):
+            t = 2 * pair + s
+            sum_copy(t, s, r).wait_recv()
+            at = pl.ds(pl.multiple_of(r * LANES, LANES), LANES)
+            to = pl.ds(pl.multiple_of(r * LANES + RIM, RIM), LANES)
+            fin[t, to] = part[t, 0, at] + from_sum[t, at] + from_one[t, at]
+
+    def finish_last(pair):
+        @pl.loop(0, 2)
+        def _(s):
+            tile_copy(2 * pair + s, s, 1).wait_recv()
+
+        finish_chunk(pair, chunks - 1)
+
+        @pl.loop(0, 2)
+        def _(s):
+            rim_copy(2 * pair + s).start()
+
+    def finish_rim(pair):
+        @pl.loop(0, 2)
+        def _(s):
+            rim_copy(2 * pair + s).wait_recv()
+
     def finish(pair):
-        @pl.loop(0, 2)
-        def _(s):
-            t = 2 * pair + s
-            tile_copy(t, s, 2).wait_recv()
-            tile_copy(t, s, 1).wait_recv()
-            last = pl.ds(rows - RIM, RIM)
-            fin[t, pl.ds(rows, RIM)] = part[t, 0, last] + from_sum[t, last] + from_one[t, last]
-            rim_copy(t).start()
-
-            @pl.loop(0, rows // LANES - 1)
-            def _(r):
-                at = pl.ds(pl.multiple_of(r * LANES, LANES), LANES)
-                to = pl.ds(pl.multiple_of(r * LANES + RIM, RIM), LANES)
-                fin[t, to] = part[t, 0, at] + from_sum[t, at] + from_one[t, at]
-
-            at = pl.ds(rows - LANES, LANES - RIM)
-            fin[t, pl.ds(rows - LANES + RIM, LANES - RIM)] = part[t, 0, at] + from_sum[t, at] + from_one[t, at]
-
-        @pl.loop(0, 2)
-        def _(s):
-            rim_copy(2 * pair + s).wait_recv()
+        finish_last(pair)
+
+        @pl.loop(1, chunks)
+        def _(i):
+            finish_chunk(pair, chunks - 1 - i)
+
+        finish_rim(pair)
 
     def shaped(t, r):
         j, g = TILES[t]
@@ -291,7 +330,7 @@
         return result
 
     def spectrum(source, g):
-        @pl.loop(0, rows // LANES)
+        @pl.loop(0, chunks)
         def _(r):
             at = pl.ds(pl.multiple_of(r * LANES, LANES), LANES)
             found = real_dft([source[g, s, :, at] for s in range(blocks)])
@@ -311,7 +350,7 @@
         work[:half] = by_cos[:half] - by_sin[half:]
         work[half:] = by_cos[half:] + by_sin[:half]
 
-        @pl.loop(0, rows // LANES)
+        @pl.loop(0, chunks)
         def _(r):
             at = pl.ds(pl.multiple_of(r * LANES, LANES), LANES)
             freq = []
@@ -323,7 +362,7 @@
                 y_sent[g, s, :, at] = value
 
     def gate(g):
-        for r in range(rows // LANES):
+        for r in range(chunks):
             at = slice(r * LANES, (r + 1) * LANES)
             u = shaped(2 * g, r) * shaped(2 * g + 1, r)
             u_kept[g, at] = u
@@ -335,11 +374,18 @@
         convolve(g)
         swap_start(2, g, y_sent, y_got)
 
-    pl.semaphore_wait(barrier, peers + 2)
+    def result(r):
+        at = pl.ds(pl.multiple_of(r * LANES, LANES), LANES)
+        for g in range(2):
+            out_ref[at, g * wide : (g + 1) * wide] = shaped(4 + g, r) * u_kept[g, at]
+        pltpu.make_async_copy(out_ref.at[at], out_hbm.at[at], out_sem.at[r]).start()
+
+    x_copy.wait()
     send_far(0)
     send_one(0)
+    h_copy.wait()
     for g in range(2):
-        for r in range(rows // LANES):
+        for r in range(chunks):
             at = slice(r * LANES, (r + 1) * LANES)
             h_sent[g, :, at] = h_ref[at, g * wide : (g + 1) * wide].T
         swap_start(0, g, h_sent, h_got)
@@ -368,15 +414,28 @@
     through(0)
     finish(1)
     gate(1)
+    send_sum(2)
     through(1)
-    send_sum(2)
-    finish(2)
     for g in range(2):
         swap_wait(swap_recv, 2, g)
-        for r in range(rows // LANES):
+        for r in range(chunks):
             at = slice(r * LANES, (r + 1) * LANES)
-            gain = gain_ref[:, g * wide : (g + 1) * wide]
-            out_ref[at, g * wide : (g + 1) * wide] = shaped(4 + g, r) * (y_got[g, :, at].T + gain * u_kept[g, at])
+            u_kept[g, at] = y_got[g, :, at].T + gain_ref[:, g * wide : (g + 1) * wide] * u_kept[g, at]
+    finish_last(2)
+
+    @pl.loop(1, chunks)
+    def _(i):
+        r = chunks - 1 - i
+        finish_chunk(2, r)
+        result(r + 1)
+
+    finish_rim(2)
+    result(0)
+
+    @pl.loop(0, chunks)
+    def _(r):
+        at = pl.ds(pl.multiple_of(r * LANES, LANES), LANES)
+        pltpu.make_async_copy(out_ref.at[at], out_hbm.at[at], out_sem.at[r]).wait()
 
     @pl.loop(0, tiles // 2)
     def _(pair):
@@ -384,8 +443,12 @@
         def _(s):
             t = 2 * pair + s
             rim_copy(t).wait_send()
-            for kind in range(3):
+            for kind in range(2):
                 tile_copy(t, s, kind).wait_send()
+
+            @pl.loop(0, chunks)
+            def _(r):
+                sum_copy(t, s, r).wait_send()
 
     for which in range(3):
         for g in range(2):
@@ -408,9 +471,12 @@
     return pl.pallas_call(
         functools.partial(kernel, blocks),
         out_shape=jax.ShapeDtypeStruct((rows, channels), F32),
-        in_specs=[vmem, hbm, vmem, vmem, vmem, hbm, vmem],
-        out_specs=vmem,
+        in_specs=[hbm, hbm, vmem, hbm, vmem, hbm, vmem],
+        out_specs=hbm,
         scratch_shapes=[
+            pltpu.VMEM((rows, depth), BF16),
+            pltpu.VMEM((rows, channels), F32),
+            pltpu.VMEM((rows, channels), F32),
             pltpu.VMEM((tiles, 4, depth, wide), BF16),
             pltpu.VMEM((4, rows, rows), BF16),
             pltpu.VMEM((tiles, 4, rows, wide), F32),
@@ -428,9 +494,12 @@
             pltpu.VMEM((2, 2 * freqs * per, rows), F32),
             pltpu.VMEM((2 * freqs * per, rows), F32),
             pltpu.SemaphoreType.DMA((tiles, 4)),
-            pltpu.SemaphoreType.DMA,
-            pltpu.SemaphoreType.DMA((3, tiles)),
-            pltpu.SemaphoreType.DMA((3, tiles)),
+            pltpu.SemaphoreType.DMA((3,)),
+            pltpu.SemaphoreType.DMA((rows // LANES,)),
+            pltpu.SemaphoreType.DMA((tiles, rows // LANES)),
+            pltpu.SemaphoreType.DMA((tiles, rows // LANES)),
+            pltpu.SemaphoreType.DMA((2, tiles)),
+            pltpu.SemaphoreType.DMA((2, tiles)),
             pltpu.SemaphoreType.DMA((tiles,)),
             pltpu.SemaphoreType.DMA((tiles,)),
             pltpu.SemaphoreType.DMA((3, 2)),

time: 121 us -> 118 us (0.975)
  Pallas kernels: 118 us -> 115 us
    pallas_call x1, Pallas kernels: 118 us -> 115 us  [on_device(): pl.pallas_call(functools.partial(kernel, blocks), out_shape=jax.ShapeDtyp...]
where the time goes in v3:
time: 118 us; the launch traced here: 117 us
  Pallas kernels  115 us (97%)
  local copies, waits for them, and re-layouts  2.26 us (2%)
    pallas_call x1, Pallas kernels, on_device(): pl.pallas_call(functools.partial(kernel, blocks), out_shape=jax.ShapeDtyp...  115 us

profile of v3, /device:TPU:0, one launch (start us, length us, event | category | flops | bytes accessed | tf_op | source)
XLA Modules:
  0.0 117.2 jit_solution(18217730899803237368)
XLA Ops:
  0.0 114.9 %shard_map.73 = f32[512,512]{1,0:T(8,128)} custom-call(bf16[512,1024]{1,0:T(8,128)(2,1)} %x_hbm.1, bf16[3,1024,2048]{2,1,0:T(8,128)(2,1)} %bitcast.2, f32[3,3,512]{2,1,0:T(4,128)} %taps_ref.1, f32[512,512]{1,0:T(8,128)} %h_hbm.1, f32[1,512]{1,0:T(1,128)} %bitcast.3, bf16[4,512,512]{2,1,0:T(8,128)(2,1)} %constant.4.clone.table_hbm, ...), custom_call_target="tpu_custom_call" | custom-call | flops 6442450944 | bytes 16777216 | tf_op jit(solution)/shard_map/pallas_call | solution.py:471
  114.9 2.3 %copy.9 = f32[512,512]{1,0:T(8,128)} copy(f32[512,512]{1,0:T(8,128)} %shard_map.73) | data formatting | bytes 2097152

commit v4 on v3

--- a/solution.py
+++ b/solution.py
@@ -127,6 +127,7 @@
     out_sem,
     sum_send,
     sum_recv,
+    here_sem,
     tile_send,
     tile_recv,
     rim_send,
@@ -142,12 +143,23 @@
     half = freqs * per
     tiles = len(TILES)
     peers = blocks - 1
+    levels = peers.bit_length()
 
     def at_col(offset):
         return (me, lax.rem(row + offset, 4))
 
     def peer(i):
         return lax.rem(me + i, blocks)
+
+    def across(level):
+        step = 1 << level
+        return (me + step - 2 * step * lax.rem(me // step, 2), row)
+
+    def meet(level):
+        if level > 0:
+            pl.semaphore_wait(here_sem.at[level - 1], 1)
+        if level < levels:
+            pl.semaphore_signal(here_sem.at[level], inc=1, device_id=across(level), device_id_type=MESH)
 
     def weight_copy(t, o):
         j, g = TILES[t]
@@ -156,12 +168,10 @@
 
     barrier = pltpu.get_barrier_semaphore()
 
-    @pl.loop(1, blocks)
-    def _(i):
-        pl.semaphore_signal(barrier, inc=1, device_id=(peer(i), row), device_id_type=MESH)
-
     for offset in (1, 3):
         pl.semaphore_signal(barrier, inc=1, device_id=at_col(offset), device_id_type=MESH)
+    for level in range(levels):
+        pl.semaphore_signal(barrier, inc=1, device_id=across(level), device_id_type=MESH)
 
     x_copy = pltpu.make_async_copy(x_hbm, x_ref, side_sem.at[0])
     h_copy = pltpu.make_async_copy(h_hbm, h_ref, side_sem.at[1])
@@ -210,7 +220,8 @@
 
                 @pl.when(s == 0)
                 def _():
-                    pl.semaphore_wait(barrier, peers + 2)
+                    pl.semaphore_wait(barrier, levels + 2)
+                    meet(0)
 
             tile_copy(2 * pair + s, s, 0).start()
 
@@ -382,15 +393,21 @@
 
     x_copy.wait()
     send_far(0)
+    meet(1)
     send_one(0)
+    meet(2)
     h_copy.wait()
     for g in range(2):
         for r in range(chunks):
             at = slice(r * LANES, (r + 1) * LANES)
             h_sent[g, :, at] = h_ref[at, g * wide : (g + 1) * wide].T
+    meet(3)
+    project_rest(0)
+    meet(4)
+    send_sum(0)
+    meet(5)
+    for g in range(2):
         swap_start(0, g, h_sent, h_got)
-    project_rest(0)
-    send_sum(0)
     send_far(1)
     send_one(1)
     project_rest(1)
@@ -498,6 +515,7 @@
             pltpu.SemaphoreType.DMA((rows // LANES,)),
             pltpu.SemaphoreType.DMA((tiles, rows // LANES)),
             pltpu.SemaphoreType.DMA((tiles, rows // LANES)),
+            pltpu.SemaphoreType.REGULAR((blocks.bit_length() - 1,)),
             pltpu.SemaphoreType.DMA((2, tiles)),
             pltpu.SemaphoreType.DMA((2, tiles)),
             pltpu.SemaphoreType.DMA((tiles,)),

time: 118 us -> 116 us (0.983)
  Pallas kernels: 115 us -> 113 us
    pallas_call x1, Pallas kernels: 115 us -> 113 us  [on_device(): pl.pallas_call(functools.partial(kernel, blocks), out_shape=jax.ShapeDtyp...]
where the time goes in v4:
time: 116 us
  Pallas kernels  113 us (97%)
  local copies, waits for them, and re-layouts  2.26 us (2%)
    pallas_call x1, Pallas kernels, on_device(): pl.pallas_call(functools.partial(kernel, blocks), out_shape=jax.ShapeDtyp...  113 us

profile of v4, /device:TPU:0, one launch (start us, length us, event | category | flops | bytes accessed | tf_op | source)
XLA Modules:
  0.0 115.5 jit_solution(13107481480804675884)
XLA Ops:
  0.0 113.2 %shard_map.73 = f32[512,512]{1,0:T(8,128)} custom-call(bf16[512,1024]{1,0:T(8,128)(2,1)} %x_hbm.1, bf16[3,1024,2048]{2,1,0:T(8,128)(2,1)} %bitcast.2, f32[3,3,512]{2,1,0:T(4,128)} %taps_ref.1, f32[512,512]{1,0:T(8,128)} %h_hbm.1, f32[1,512]{1,0:T(1,128)} %bitcast.3, bf16[4,512,512]{2,1,0:T(8,128)(2,1)} %constant.4.clone.table_hbm, ...), custom_call_target="tpu_custom_call" | custom-call | flops 6442450944 | bytes 16777216 | tf_op jit(solution)/shard_map/pallas_call | solution.py:488
  113.2 2.3 %copy.9 = f32[512,512]{1,0:T(8,128)} copy(f32[512,512]{1,0:T(8,128)} %shard_map.73) | data formatting | bytes 2097152

commit v5 on v4

--- a/solution.py
+++ b/solution.py
@@ -97,15 +97,17 @@
     blocks,
     x_hbm,
     w_hbm,
+    taps_hbm,
+    h_hbm,
+    gain_hbm,
+    table_hbm,
+    turn_hbm,
+    out_ref,
+    x_ref,
     taps_ref,
-    h_hbm,
+    h_ref,
     gain_ref,
-    table_hbm,
     turn_ref,
-    out_hbm,
-    x_ref,
-    h_ref,
-    out_ref,
     w_vm,
     table,
     part,
@@ -124,7 +126,8 @@
     work,
     w_sem,
     side_sem,
-    out_sem,
+    far_send,
+    far_recv,
     sum_send,
     sum_recv,
     here_sem,
@@ -166,24 +169,26 @@
         start = pl.multiple_of(lax.rem(row + o, 4) * (2 * wide) + g * wide, LANES)
         return pltpu.make_async_copy(w_hbm.at[j, :, pl.ds(start, wide)], w_vm.at[t, o], w_sem.at[t, o])
 
+    operands = ((x_hbm, x_ref), (h_hbm, h_ref), (taps_hbm, taps_ref), (table_hbm, table), (turn_hbm, turn_ref), (gain_hbm, gain_ref))
+    x_copy, h_copy, *side_copies = [
+        pltpu.make_async_copy(src, dst, side_sem.at[i]) for i, (src, dst) in enumerate(operands)
+    ]
+    x_copy.start()
+    weight_copy(0, 2).start()
+    weight_copy(1, 2).start()
     barrier = pltpu.get_barrier_semaphore()
-
     for offset in (1, 3):
         pl.semaphore_signal(barrier, inc=1, device_id=at_col(offset), device_id_type=MESH)
     for level in range(levels):
         pl.semaphore_signal(barrier, inc=1, device_id=across(level), device_id_type=MESH)
-
-    x_copy = pltpu.make_async_copy(x_hbm, x_ref, side_sem.at[0])
-    h_copy = pltpu.make_async_copy(h_hbm, h_ref, side_sem.at[1])
-    table_copy = pltpu.make_async_copy(table_hbm, table, side_sem.at[2])
-    x_copy.start()
-    for pair in range(tiles // 2):
+    weight_copy(0, 3).start()
+    weight_copy(1, 1).start()
+
+    def fetch(pair):
         for order in ((2, 2), (3, 1), (1, 3), (0, 0)):
             for s in range(2):
-                weight_copy(2 * pair + s, order[s]).start()
-        if pair == 0:
-            h_copy.start()
-    table_copy.start()
+                if pair > 0 or order[0] < 2:
+                    weight_copy(2 * pair + s, order[s]).start()
 
     def project(t, o):
         pltpu.make_async_copy(w_vm.at[t, o], w_vm.at[t, o], w_sem.at[t, o]).wait()
@@ -212,17 +217,38 @@
             device_id_type=MESH,
         )
 
+    def far_copy(t, s, r):
+        at = pl.ds(pl.multiple_of(r * LANES, LANES), LANES)
+        return pltpu.make_async_remote_copy(
+            src_ref=part.at[t, 2, at],
+            dst_ref=relay.at[t, at],
+            send_sem=far_send.at[t, r],
+            recv_sem=far_recv.at[t, r],
+            device_id=at_col(1 + 2 * s),
+            device_id_type=MESH,
+        )
+
+    def send_first():
+        for s in range(2):
+            pltpu.make_async_copy(w_vm.at[s, 2], w_vm.at[s, 2], w_sem.at[s, 2]).wait()
+
+        @pl.loop(0, 2 * chunks)
+        def _(i):
+            r, s = i // 2, lax.rem(i, 2)
+            at = pl.ds(pl.multiple_of(r * LANES, LANES), LANES)
+            part[s, 2, at] = jnp.dot(x_ref[at, :], w_vm[s, 2], preferred_element_type=F32)
+
+            @pl.when(i == 0)
+            def _():
+                pl.semaphore_wait(barrier, levels + 2)
+                meet(0)
+
+            far_copy(s, s, r).start()
+
     def send_far(pair):
         @pl.loop(0, 2)
         def _(s):
             project(2 * pair + s, 2)
-            if pair == 0:
-
-                @pl.when(s == 0)
-                def _():
-                    pl.semaphore_wait(barrier, levels + 2)
-                    meet(0)
-
             tile_copy(2 * pair + s, s, 0).start()
 
     def send_one(pair):
@@ -238,9 +264,18 @@
             project(2 * pair + s, 0)
 
     def send_sum(pair):
-        @pl.loop(0, 2)
-        def _(s):
-            tile_copy(2 * pair + s, s, 0).wait_recv()
+        if pair > 0:
+
+            @pl.loop(0, 2)
+            def _(s):
+                tile_copy(2 * pair + s, s, 0).wait_recv()
+
+        else:
+
+            @pl.loop(0, chunks)
+            def _(r):
+                for s in range(2):
+                    far_copy(s, s, r).wait_recv()
 
         @pl.loop(0, chunks)
         def _(i):
@@ -389,13 +424,15 @@
         at = pl.ds(pl.multiple_of(r * LANES, LANES), LANES)
         for g in range(2):
             out_ref[at, g * wide : (g + 1) * wide] = shaped(4 + g, r) * u_kept[g, at]
-        pltpu.make_async_copy(out_ref.at[at], out_hbm.at[at], out_sem.at[r]).start()
 
     x_copy.wait()
-    send_far(0)
+    send_first()
     meet(1)
     send_one(0)
+    h_copy.start()
+    fetch(0)
     meet(2)
+    fetch(1)
     h_copy.wait()
     for g in range(2):
         for r in range(chunks):
@@ -404,14 +441,18 @@
     meet(3)
     project_rest(0)
     meet(4)
+    for copy in side_copies:
+        copy.start()
     send_sum(0)
     meet(5)
     for g in range(2):
         swap_start(0, g, h_sent, h_got)
+    fetch(2)
     send_far(1)
     send_one(1)
     project_rest(1)
-    table_copy.wait()
+    for copy in side_copies:
+        copy.wait()
     scale = 1.0 / (blocks * rows)
     for g in range(2):
         swap_wait(swap_recv, 0, g)
@@ -451,8 +492,8 @@
 
     @pl.loop(0, chunks)
     def _(r):
-        at = pl.ds(pl.multiple_of(r * LANES, LANES), LANES)
-        pltpu.make_async_copy(out_ref.at[at], out_hbm.at[at], out_sem.at[r]).wait()
+        for s in range(2):
+            far_copy(s, s, r).wait_send()
 
     @pl.loop(0, tiles // 2)
     def _(pair):
@@ -460,8 +501,11 @@
         def _(s):
             t = 2 * pair + s
             rim_copy(t).wait_send()
-            for kind in range(2):
-                tile_copy(t, s, kind).wait_send()
+            tile_copy(t, s, 1).wait_send()
+
+            @pl.when(pair > 0)
+            def _():
+                tile_copy(t, s, 0).wait_send()
 
             @pl.loop(0, chunks)
             def _(r):
@@ -487,13 +531,15 @@
     flipped = (2, wide, rows)
     return pl.pallas_call(
         functools.partial(kernel, blocks),
-        out_shape=jax.ShapeDtypeStruct((rows, channels), F32),
-        in_specs=[hbm, hbm, vmem, hbm, vmem, hbm, vmem],
-        out_specs=hbm,
+        out_shape=pltpu.VMEM((rows, channels), F32),
+        in_specs=[hbm] * 7,
+        out_specs=vmem,
         scratch_shapes=[
             pltpu.VMEM((rows, depth), BF16),
+            pltpu.VMEM(short_filter.shape, F32),
             pltpu.VMEM((rows, channels), F32),
-            pltpu.VMEM((rows, channels), F32),
+            pltpu.VMEM((1, channels), F32),
+            pltpu.VMEM((2, freqs, rows), F32),
             pltpu.VMEM((tiles, 4, depth, wide), BF16),
             pltpu.VMEM((4, rows, rows), BF16),
             pltpu.VMEM((tiles, 4, rows, wide), F32),
@@ -511,8 +557,9 @@
             pltpu.VMEM((2, 2 * freqs * per, rows), F32),
             pltpu.VMEM((2 * freqs * per, rows), F32),
             pltpu.SemaphoreType.DMA((tiles, 4)),
-            pltpu.SemaphoreType.DMA((3,)),
-            pltpu.SemaphoreType.DMA((rows // LANES,)),
+            pltpu.SemaphoreType.DMA((6,)),
+            pltpu.SemaphoreType.DMA((2, rows // LANES)),
+            pltpu.SemaphoreType.DMA((2, rows // LANES)),
             pltpu.SemaphoreType.DMA((tiles, rows // LANES)),
             pltpu.SemaphoreType.DMA((tiles, rows // LANES)),
             pltpu.SemaphoreType.REGULAR((blocks.bit_length() - 1,)),
@@ -524,7 +571,7 @@
             pltpu.SemaphoreType.DMA((3, 2)),
         ],
         compiler_params=pltpu.CompilerParams(
-            collective_id=0, has_side_effects=True, vmem_limit_bytes=60 << 20
+            collective_id=0, has_side_effects=True, vmem_limit_bytes=56 << 20
         ),
         cost_estimate=pl.CostEstimate(
             flops=2 * rows * depth * 12 * channels, bytes_accessed=16 << 20, transcendentals=0

time: 116 us -> 111 us (0.957)
  Pallas kernels: 113 us -> 110 us
  local copies, waits for them, and re-layouts: 2.26 us -> 0.97 us
    pallas_call x1, Pallas kernels: 113 us -> 110 us  [on_device(): pl.pallas_call(functools.partial(kernel, blocks), out_shape=pltpu.VMEM((r...]
    unnamed x1, local copies, waits for them, and re-layouts: 2.26 us -> 0.97 us
where the time goes in v5:
time: 111 us
  Pallas kernels  110 us (99%)
    pallas_call x1, Pallas kernels, on_device(): pl.pallas_call(functools.partial(kernel, blocks), out_shape=pltpu.VMEM((r...  110 us

profile of v5, /device:TPU:0, one launch (start us, length us, event | category | flops | bytes accessed | tf_op | source)
XLA Modules:
  0.0 111.3 jit_solution(12342415858129292665)
XLA Ops:
  0.0 110.3 %shard_map.73 = f32[512,512]{1,0:T(8,128)S(1)} custom-call(bf16[512,1024]{1,0:T(8,128)(2,1)} %x_hbm.1, bf16[3,1024,2048]{2,1,0:T(8,128)(2,1)} %bitcast.2, f32[3,3,512]{2,1,0:T(4,128)} %taps_hbm.1, f32[512,512]{1,0:T(8,128)} %h_hbm.1, f32[1,512]{1,0:T(1,128)} %bitcast.3, bf16[4,512,512]{2,1,0:T(8,128)(2,1)} %constant.4.clone.table_hbm, ...), custom_call_target="tpu_custom_call" | custom-call | flops 6442450944 | bytes 16777216 | tf_op jit(solution)/shard_map/pallas_call | solution.py:532
  110.3 1.0 copy.9

commit v6 on v5

--- a/solution.py
+++ b/solution.py
@@ -146,7 +146,7 @@
     half = freqs * per
     tiles = len(TILES)
     peers = blocks - 1
-    levels = peers.bit_length()
+    levels = blocks.bit_length() - 2
 
     def at_col(offset):
         return (me, lax.rem(row + offset, 4))
@@ -154,15 +154,12 @@
     def peer(i):
         return lax.rem(me + i, blocks)
 
-    def across(level):
-        step = 1 << level
-        return (me + step - 2 * step * lax.rem(me // step, 2), row)
-
     def meet(level):
         if level > 0:
-            pl.semaphore_wait(here_sem.at[level - 1], 1)
+            pl.semaphore_wait(here_sem.at[level - 1], 2)
         if level < levels:
-            pl.semaphore_signal(here_sem.at[level], inc=1, device_id=across(level), device_id_type=MESH)
+            for offset in (1 << level, blocks - (1 << level)):
+                pl.semaphore_signal(here_sem.at[level], inc=1, device_id=(peer(offset), row), device_id_type=MESH)
 
     def weight_copy(t, o):
         j, g = TILES[t]
@@ -179,8 +176,8 @@
     barrier = pltpu.get_barrier_semaphore()
     for offset in (1, 3):
         pl.semaphore_signal(barrier, inc=1, device_id=at_col(offset), device_id_type=MESH)
-    for level in range(levels):
-        pl.semaphore_signal(barrier, inc=1, device_id=across(level), device_id_type=MESH)
+    for offset in (1, peers):
+        pl.semaphore_signal(barrier, inc=1, device_id=(peer(offset), row), device_id_type=MESH)
     weight_copy(0, 3).start()
     weight_copy(1, 1).start()
 
@@ -240,8 +237,7 @@
 
             @pl.when(i == 0)
             def _():
-                pl.semaphore_wait(barrier, levels + 2)
-                meet(0)
+                pl.semaphore_wait(barrier, 4)
 
             far_copy(s, s, r).start()
 
@@ -420,6 +416,19 @@
         convolve(g)
         swap_start(2, g, y_sent, y_got)
 
+    def sent(pair):
+        @pl.loop(0, 2)
+        def _(s):
+            t = 2 * pair + s
+            if pair > 0:
+                tile_copy(t, s, 0).wait_send()
+            tile_copy(t, s, 1).wait_send()
+            rim_copy(t).wait_send()
+
+            @pl.loop(0, chunks)
+            def _(r):
+                sum_copy(t, s, r).wait_send()
+
     def result(r):
         at = pl.ds(pl.multiple_of(r * LANES, LANES), LANES)
         for g in range(2):
@@ -427,24 +436,24 @@
 
     x_copy.wait()
     send_first()
-    meet(1)
+    meet(0)
     send_one(0)
     h_copy.start()
     fetch(0)
-    meet(2)
+    meet(1)
     fetch(1)
     h_copy.wait()
     for g in range(2):
         for r in range(chunks):
             at = slice(r * LANES, (r + 1) * LANES)
             h_sent[g, :, at] = h_ref[at, g * wide : (g + 1) * wide].T
+    meet(2)
+    project_rest(0)
     meet(3)
-    project_rest(0)
-    meet(4)
     for copy in side_copies:
         copy.start()
     send_sum(0)
-    meet(5)
+    meet(4)
     for g in range(2):
         swap_start(0, g, h_sent, h_got)
     fetch(2)
@@ -479,6 +488,16 @@
         for r in range(chunks):
             at = slice(r * LANES, (r + 1) * LANES)
             u_kept[g, at] = y_got[g, :, at].T + gain_ref[:, g * wide : (g + 1) * wide] * u_kept[g, at]
+    @pl.loop(0, chunks)
+    def _(r):
+        for s in range(2):
+            far_copy(s, s, r).wait_send()
+
+    sent(0)
+    sent(1)
+    for which in range(3):
+        for g in range(2):
+            swap_wait(swap_send, which, g)
     finish_last(2)
 
     @pl.loop(1, chunks)
@@ -490,30 +509,7 @@
     finish_rim(2)
     result(0)
 
-    @pl.loop(0, chunks)
-    def _(r):
-        for s in range(2):
-            far_copy(s, s, r).wait_send()
-
-    @pl.loop(0, tiles // 2)
-    def _(pair):
-        @pl.loop(0, 2)
-        def _(s):
-            t = 2 * pair + s
-            rim_copy(t).wait_send()
-            tile_copy(t, s, 1).wait_send()
-
-            @pl.when(pair > 0)
-            def _():
-                tile_copy(t, s, 0).wait_send()
-
-            @pl.loop(0, chunks)
-            def _(r):
-                sum_copy(t, s, r).wait_send()
-
-    for which in range(3):
-        for g in range(2):
-            swap_wait(swap_send, which, g)
+    sent(2)
 
 
 def on_device(blocks, sequence, w_proj, short_filter, long_filter, skip_gain):
@@ -562,7 +558,7 @@
             pltpu.SemaphoreType.DMA((2, rows // LANES)),
             pltpu.SemaphoreType.DMA((tiles, rows // LANES)),
             pltpu.SemaphoreType.DMA((tiles, rows // LANES)),
-            pltpu.SemaphoreType.REGULAR((blocks.bit_length() - 1,)),
+            pltpu.SemaphoreType.REGULAR((blocks.bit_length() - 2,)),
             pltpu.SemaphoreType.DMA((2, tiles)),
             pltpu.SemaphoreType.DMA((2, tiles)),
             pltpu.SemaphoreType.DMA((tiles,)),

time: 111 us -> 110 us (level)
  Pallas kernels: 110 us -> 108 us
    pallas_call x1, Pallas kernels: 110 us -> 108 us  [on_device(): pl.pallas_call(functools.partial(kernel, blocks), out_shape=pltpu.VMEM((r...]
where the time goes in v6:
time: 110 us; the launch traced here: 109 us
  Pallas kernels  108 us (98%)
    pallas_call x1, Pallas kernels, on_device(): pl.pallas_call(functools.partial(kernel, blocks), out_shape=pltpu.VMEM((r...  108 us

profile of v6, /device:TPU:0, one launch (start us, length us, event | category | flops | bytes accessed | tf_op | source)
XLA Modules:
  0.0 109.3 jit_solution(18115161940140560042)
XLA Ops:
  0.0 108.3 %shard_map.73 = f32[512,512]{1,0:T(8,128)S(1)} custom-call(bf16[512,1024]{1,0:T(8,128)(2,1)} %x_hbm.1, bf16[3,1024,2048]{2,1,0:T(8,128)(2,1)} %bitcast.2, f32[3,3,512]{2,1,0:T(4,128)} %taps_hbm.1, f32[512,512]{1,0:T(8,128)} %h_hbm.1, f32[1,512]{1,0:T(1,128)} %bitcast.3, bf16[4,512,512]{2,1,0:T(8,128)(2,1)} %constant.4.clone.table_hbm, ...), custom_call_target="tpu_custom_call" | custom-call | flops 6442450944 | bytes 16777216 | tf_op jit(solution)/shard_map/pallas_call | solution.py:528
  108.3 1.0 copy.9

commit v7 on v6

--- a/solution.py
+++ b/solution.py
@@ -125,6 +125,7 @@
     h_freq,
     work,
     w_sem,
+    x_sem,
     side_sem,
     far_send,
     far_recv,
@@ -146,7 +147,7 @@
     half = freqs * per
     tiles = len(TILES)
     peers = blocks - 1
-    levels = blocks.bit_length() - 2
+    levels = blocks.bit_length() - 1
 
     def at_col(offset):
         return (me, lax.rem(row + offset, 4))
@@ -155,29 +156,49 @@
         return lax.rem(me + i, blocks)
 
     def meet(level):
+        def tell(offset):
+            pl.semaphore_signal(
+                here_sem.at[level], inc=1, device_id=(peer(offset), row), device_id_type=MESH
+            )
+
         if level > 0:
-            pl.semaphore_wait(here_sem.at[level - 1], 2)
-        if level < levels:
-            for offset in (1 << level, blocks - (1 << level)):
-                pl.semaphore_signal(here_sem.at[level], inc=1, device_id=(peer(offset), row), device_id_type=MESH)
+            pl.semaphore_wait(here_sem.at[level - 1], 1 if level == 1 else 2)
+        if level == 0:
+            tell(peers)
+        elif level < levels:
+            tell(1 << (level - 1))
+            tell(blocks - (1 << (level - 1)))
 
     def weight_copy(t, o):
         j, g = TILES[t]
         start = pl.multiple_of(lax.rem(row + o, 4) * (2 * wide) + g * wide, LANES)
         return pltpu.make_async_copy(w_hbm.at[j, :, pl.ds(start, wide)], w_vm.at[t, o], w_sem.at[t, o])
 
-    operands = ((x_hbm, x_ref), (h_hbm, h_ref), (taps_hbm, taps_ref), (table_hbm, table), (turn_hbm, turn_ref), (gain_hbm, gain_ref))
-    x_copy, h_copy, *side_copies = [
+    def x_copy(r):
+        at = pl.ds(pl.multiple_of(r * LANES, LANES), LANES)
+        return pltpu.make_async_copy(x_hbm.at[at], x_ref.at[at], x_sem.at[r])
+
+    def weight_pieces(t, o):
+        j, g = TILES[t]
+        start = pl.multiple_of(lax.rem(row + o, 4) * (2 * wide) + g * wide, LANES)
+        deep = x_ref.shape[1] // 4
+        for i in range(4):
+            at = pl.ds(i * deep, deep)
+            pltpu.make_async_copy(w_hbm.at[j, at, pl.ds(start, wide)], w_vm.at[t, o, at], w_sem.at[t, o]).start()
+
+    operands = ((h_hbm, h_ref), (taps_hbm, taps_ref), (table_hbm, table), (turn_hbm, turn_ref), (gain_hbm, gain_ref))
+    h_copy, *side_copies = [
         pltpu.make_async_copy(src, dst, side_sem.at[i]) for i, (src, dst) in enumerate(operands)
     ]
-    x_copy.start()
-    weight_copy(0, 2).start()
-    weight_copy(1, 2).start()
+    x_copy(0).start()
+    weight_pieces(0, 2)
+    weight_pieces(1, 2)
+    for r in range(1, chunks):
+        x_copy(r).start()
     barrier = pltpu.get_barrier_semaphore()
     for offset in (1, 3):
         pl.semaphore_signal(barrier, inc=1, device_id=at_col(offset), device_id_type=MESH)
-    for offset in (1, peers):
-        pl.semaphore_signal(barrier, inc=1, device_id=(peer(offset), row), device_id_type=MESH)
+    pl.semaphore_signal(barrier, inc=1, device_id=(peer(1), row), device_id_type=MESH)
     weight_copy(0, 3).start()
     weight_copy(1, 1).start()
 
@@ -226,18 +247,24 @@
         )
 
     def send_first():
-        for s in range(2):
-            pltpu.make_async_copy(w_vm.at[s, 2], w_vm.at[s, 2], w_sem.at[s, 2]).wait()
-
         @pl.loop(0, 2 * chunks)
         def _(i):
             r, s = i // 2, lax.rem(i, 2)
             at = pl.ds(pl.multiple_of(r * LANES, LANES), LANES)
+
+            @pl.when(r == 0)
+            def _():
+                pltpu.make_async_copy(w_vm.at[s, 2], w_vm.at[s, 2], w_sem.at[s, 2]).wait()
+
+            @pl.when(s == 0)
+            def _():
+                x_copy(r).wait()
+
             part[s, 2, at] = jnp.dot(x_ref[at, :], w_vm[s, 2], preferred_element_type=F32)
 
             @pl.when(i == 0)
             def _():
-                pl.semaphore_wait(barrier, 4)
+                pl.semaphore_wait(barrier, 3)
 
             far_copy(s, s, r).start()
 
@@ -434,26 +461,26 @@
         for g in range(2):
             out_ref[at, g * wide : (g + 1) * wide] = shaped(4 + g, r) * u_kept[g, at]
 
-    x_copy.wait()
     send_first()
     meet(0)
+    meet(1)
     send_one(0)
     h_copy.start()
     fetch(0)
-    meet(1)
+    meet(2)
     fetch(1)
     h_copy.wait()
     for g in range(2):
         for r in range(chunks):
             at = slice(r * LANES, (r + 1) * LANES)
             h_sent[g, :, at] = h_ref[at, g * wide : (g + 1) * wide].T
-    meet(2)
+    meet(3)
     project_rest(0)
-    meet(3)
+    meet(4)
     for copy in side_copies:
         copy.start()
     send_sum(0)
-    meet(4)
+    meet(5)
     for g in range(2):
         swap_start(0, g, h_sent, h_got)
     fetch(2)
@@ -553,12 +580,13 @@
             pltpu.VMEM((2, 2 * freqs * per, rows), F32),
             pltpu.VMEM((2 * freqs * per, rows), F32),
             pltpu.SemaphoreType.DMA((tiles, 4)),
-            pltpu.SemaphoreType.DMA((6,)),
+            pltpu.SemaphoreType.DMA((rows // LANES,)),
+            pltpu.SemaphoreType.DMA((5,)),
             pltpu.SemaphoreType.DMA((2, rows // LANES)),
             pltpu.SemaphoreType.DMA((2, rows // LANES)),
             pltpu.SemaphoreType.DMA((tiles, rows // LANES)),
             pltpu.SemaphoreType.DMA((tiles, rows // LANES)),
-            pltpu.SemaphoreType.REGULAR((blocks.bit_length() - 2,)),
+            pltpu.SemaphoreType.REGULAR((blocks.bit_length() - 1,)),
             pltpu.SemaphoreType.DMA((2, tiles)),
             pltpu.SemaphoreType.DMA((2, tiles)),
             pltpu.SemaphoreType.DMA((tiles,)),

time: 110 us -> 109 us (level)
  no operation moved by 1% of the time
where the time goes in v7:
time: 109 us
  Pallas kernels  108 us (99%)
    pallas_call x1, Pallas kernels, on_device(): pl.pallas_call(functools.partial(kernel, blocks), out_shape=pltpu.VMEM((r...  108 us

profile of v7, /device:TPU:0, one launch (start us, length us, event | category | flops | bytes accessed | tf_op | source)
XLA Modules:
  0.0 109.0 jit_solution(146417045770991040)
XLA Ops:
  0.0 108.0 %shard_map.73 = f32[512,512]{1,0:T(8,128)S(1)} custom-call(bf16[512,1024]{1,0:T(8,128)(2,1)} %x_hbm.1, bf16[3,1024,2048]{2,1,0:T(8,128)(2,1)} %bitcast.2, f32[3,3,512]{2,1,0:T(4,128)} %taps_hbm.1, f32[512,512]{1,0:T(8,128)} %h_hbm.1, f32[1,512]{1,0:T(1,128)} %bitcast.3, bf16[4,512,512]{2,1,0:T(8,128)(2,1)} %constant.4.clone.table_hbm, ...), custom_call_target="tpu_custom_call" | custom-call | flops 6442450944 | bytes 16777216 | tf_op jit(solution)/shard_map/pallas_call | solution.py:555
  108.0 1.0 copy.9

commit v8 on v7

--- a/solution.py
+++ b/solution.py
@@ -190,15 +190,15 @@
     h_copy, *side_copies = [
         pltpu.make_async_copy(src, dst, side_sem.at[i]) for i, (src, dst) in enumerate(operands)
     ]
+    barrier = pltpu.get_barrier_semaphore()
+    for offset in (1, 3):
+        pl.semaphore_signal(barrier, inc=1, device_id=at_col(offset), device_id_type=MESH)
+    pl.semaphore_signal(barrier, inc=1, device_id=(peer(1), row), device_id_type=MESH)
     x_copy(0).start()
     weight_pieces(0, 2)
     weight_pieces(1, 2)
     for r in range(1, chunks):
         x_copy(r).start()
-    barrier = pltpu.get_barrier_semaphore()
-    for offset in (1, 3):
-        pl.semaphore_signal(barrier, inc=1, device_id=at_col(offset), device_id_type=MESH)
-    pl.semaphore_signal(barrier, inc=1, device_id=(peer(1), row), device_id_type=MESH)
     weight_copy(0, 3).start()
     weight_copy(1, 1).start()
 

time: 109 us -> 109 us (level)
  no operation moved by 1% of the time
where the time goes in v8:
time: 109 us
  Pallas kernels  108 us (99%)
    pallas_call x1, Pallas kernels, on_device(): pl.pallas_call(functools.partial(kernel, blocks), out_shape=pltpu.VMEM((r...  108 us

profile of v8, /device:TPU:0, one launch (start us, length us, event | category | flops | bytes accessed | tf_op | source)
XLA Modules:
  0.0 109.1 jit_solution(2424423139599705180)
XLA Ops:
  0.0 108.1 %shard_map.73 = f32[512,512]{1,0:T(8,128)S(1)} custom-call(bf16[512,1024]{1,0:T(8,128)(2,1)} %x_hbm.1, bf16[3,1024,2048]{2,1,0:T(8,128)(2,1)} %bitcast.2, f32[3,3,512]{2,1,0:T(4,128)} %taps_hbm.1, f32[512,512]{1,0:T(8,128)} %h_hbm.1, f32[1,512]{1,0:T(1,128)} %bitcast.3, bf16[4,512,512]{2,1,0:T(8,128)(2,1)} %constant.4.clone.table_hbm, ...), custom_call_target="tpu_custom_call" | custom-call | flops 6442450944 | bytes 16777216 | tf_op jit(solution)/shard_map/pallas_call | solution.py:555
  108.1 1.0 copy.9
